TPU v7x, 512 devices: a whole 4x8x8 slice. The times are simulated.
512 devices in a mesh: energy: 16 (over x, y_hi), width: 32 (over z, y_lo, core).
Axes of the slice: x: 4, y: 8 (y_hi: 4, y_lo: 2; y = y_hi * 2 + y_lo), z: 8, core: 2. Of those that a mesh axis runs over, the one named last changes fastest.
Arguments:
- inverse_blocks: bfloat16 [32, 8192, 256], P('energy', 'width')
- source: bfloat16 [32, 8192, 512], P('energy', 'width'), may hold values from -6 to 6
- left_coupling: bfloat16 [1024, 256], P('width'), may hold values from -0.875 to 0.875
- right_coupling: bfloat16 [1024, 256], P('width'), may hold values from -0.875 to 0.875
- energy_weights: float32 [32], P('energy'), may hold values from 0.25 to 2
- collector_low: int32 [32], P('width'), may hold values from 0 to 63
- collector_high: int32 [32], P('width'), may hold values from 193 to 256
Outputs:
- gradient: float32 [32, 256, 256], P('width', 'energy')
Inputs may be any that keep to these rules, and one draw needn't show every extreme that they name: collector_low < 64 and collector_high > 192 for every strip.
All inputs are finite; a program needn't handle non-finite values.
Results may differ from a plain program's by a relative error of at most 0.0033.
Values may be sent and summed in bfloat16 or wider, within the bound.
No kernel may reach another device: no remote copies, remote signals or barrier semaphores. Data moves between devices by JAX's collectives and lax.ppermute only.
A program may use at most 64 MiB of HBM per device.

v0:
```python
import jax
import jax.numpy as jnp
from jax import lax
from jax.sharding import PartitionSpec as P

SWEEPS = 10


def with_halo(block, sides, width):
    for axis, dim in sides:
        count = lax.axis_size(axis)
        forward = [(i, i + 1) for i in range(count - 1)]
        forward.append((count - 1, 0))
        backward = [(target, source) for source, target in forward]
        low = lax.ppermute(
            lax.slice_in_dim(block, block.shape[dim] - width, None, axis=dim), axis, forward
        )
        high = lax.ppermute(lax.slice_in_dim(block, 0, width, axis=dim), axis, backward)
        block = jnp.concatenate([low, block, high], axis=dim)
    return block


def couple_rows(left_coupling, right_coupling, tails, heads):
    first = jnp.einsum("ei,kem->kim", left_coupling, tails, preferred_element_type=jnp.float32)
    second = jnp.einsum("ei,kem->kim", right_coupling, heads, preferred_element_type=jnp.float32)
    return first + second


def body(
    inverse_blocks,
    source,
    left_coupling,
    right_coupling,
    energy_weights,
    collector_low,
    collector_high,
):
    edge = left_coupling.shape[0]
    block = inverse_blocks.shape[1]
    count = inverse_blocks.shape[0]
    modes = source.shape[2]
    psi = jnp.einsum(
        "kij,kjm->kim", inverse_blocks, source, preferred_element_type=jnp.float32
    ).astype(jnp.bfloat16)

    def forward_sweep(sweep, psi):
        padded = with_halo(psi, (("width", 1),), edge)
        tails = padded[:, :edge]
        heads = padded[:, padded.shape[1] - edge :]
        couple = couple_rows(left_coupling, right_coupling, tails, heads)
        rhs = (source.astype(jnp.float32) + couple).astype(jnp.bfloat16)
        return jnp.einsum(
            "kij,kjm->kim", inverse_blocks, rhs, preferred_element_type=jnp.float32
        ).astype(jnp.bfloat16)

    psi = lax.fori_loop(0, SWEEPS - 1, forward_sweep, psi)
    rows = lax.iota(jnp.int32, block)
    mask = ((rows >= collector_low[0]) & (rows < collector_high[0])).astype(jnp.float32)
    adjoint_source = (
        2.0 * energy_weights[:, None, None] * mask[None, :, None] * psi.astype(jnp.float32)
    )
    lam = jnp.einsum(
        "kji,kjm->kim",
        inverse_blocks,
        adjoint_source.astype(jnp.bfloat16),
        preferred_element_type=jnp.float32,
    ).astype(jnp.bfloat16)
    middle = jnp.zeros((count, block - 2 * edge, modes), jnp.float32)

    def adjoint_sweep(sweep, lam):
        to_prev = jnp.einsum(
            "ei,kim->kem", left_coupling, lam, preferred_element_type=jnp.float32
        ).astype(jnp.bfloat16)
        to_next = jnp.einsum(
            "ei,kim->kem", right_coupling, lam, preferred_element_type=jnp.float32
        ).astype(jnp.bfloat16)
        outgoing = jnp.concatenate([to_prev, to_next], axis=1)
        padded = with_halo(outgoing, (("width", 1),), edge)
        from_prev = padded[:, :edge]
        from_next = padded[:, padded.shape[1] - edge :]
        extra = jnp.concatenate(
            [from_prev.astype(jnp.float32), middle, from_next.astype(jnp.float32)], axis=1
        )
        update = (adjoint_source + extra).astype(jnp.bfloat16)
        return jnp.einsum(
            "kji,kjm->kim", inverse_blocks, update, preferred_element_type=jnp.float32
        ).astype(jnp.bfloat16)

    lam = lax.fori_loop(0, SWEEPS - 1, adjoint_sweep, lam)
    owned = block // lax.axis_size("energy")
    product = jnp.einsum("kim,kjm->ij", lam, psi, preferred_element_type=jnp.float32)
    full = lax.psum(product * (-1.0 / modes), "energy")
    mine = lax.dynamic_slice_in_dim(full, lax.axis_index("energy") * owned, owned, 0)
    return mine.reshape(1, owned, block)


def solution(mesh):
    placed = (
        P("energy", "width", None),
        P("energy", "width", None),
        P("width", None),
        P("width", None),
        P("energy"),
        P("width"),
        P("width"),
    )
    return jax.shard_map(
        body, mesh=mesh, in_specs=placed, out_specs=P("width", "energy", None), check_vma=False
    )
```

profile of v0, /device:TPU:8, one launch (start us, length us, event | category | flops | bytes accessed | tf_op | source)
XLA Modules:
  0.0 456.5 jit_solution(2762212867480273165)
XLA Ops:
  9.8 128.6 %while.20 = (s32[]{:T(128)}, bf16[2,256,512]{1,2,0:T(8,128)(2,1)S(1)}, bf16[2,256,512]{1,2,0:T(8,128)(2,1)S(1)}, bf16[32,256]{1,0:T(8,128)(2,1)S(1)}, bf16[32,25...) while((s32[]{:T(128)}, bf16[2,256,512]{1,2,0:T(8,128)(2,1)S(1)}, ...), condition=%wide.region_1.0_spmd, body=%wide.region_0.0_spmd.sunk | while | flops 169082880 | bytes 4358301 | solution.py:56
  10.0 1.9 collective-permute-start
  11.9 2.4 collective-permute-start.1
  16.0 8.1 %collective-permute-done.1 = bf16[2,32,512]{1,2,0:T(8,128)(2,1)S(1)} collective-permute-done((bf16[2,32,512]{1,2,0:T(8,128)(2,1)S(1)}, bf16[2,32,512]{1,2,0:T(8,128)(2,1)S(1)}, u32[]{:S(2)}, u32[]{:S(2)}) %collective-permute-start.1) | collective-permute-done | bytes 65568 | tf_op jit(solution)/shard_map/while/body/eval_jaxpr/ppermute | solution.py:15
  24.9 2.6 collective-permute-start
  27.5 1.9 collective-permute-start.1
  29.4 3.7 collective-permute-done
  33.4 8.0 %collective-permute-done.1 = bf16[2,32,512]{1,2,0:T(8,128)(2,1)S(1)} collective-permute-done((bf16[2,32,512]{1,2,0:T(8,128)(2,1)S(1)}, bf16[2,32,512]{1,2,0:T(8,128)(2,1)S(1)}, u32[]{:S(2)}, u32[]{:S(2)}) %collective-permute-start.1) | collective-permute-done | bytes 65568 | tf_op jit(solution)/shard_map/while/body/eval_jaxpr/ppermute | solution.py:15
  42.1 1.9 collective-permute-start
  44.0 2.4 collective-permute-start.1
  46.4 2.5 collective-permute-done
  49.2 4.7 %collective-permute-done.1 = bf16[2,32,512]{1,2,0:T(8,128)(2,1)S(1)} collective-permute-done((bf16[2,32,512]{1,2,0:T(8,128)(2,1)S(1)}, bf16[2,32,512]{1,2,0:T(8,128)(2,1)S(1)}, u32[]{:S(2)}, u32[]{:S(2)}) %collective-permute-start.1) | collective-permute-done | bytes 65568 | tf_op jit(solution)/shard_map/while/body/eval_jaxpr/ppermute | solution.py:15
  54.5 1.9 collective-permute-start
  56.5 2.4 collective-permute-start.1
  58.9 2.5 collective-permute-done
  61.6 4.7 %collective-permute-done.1 = bf16[2,32,512]{1,2,0:T(8,128)(2,1)S(1)} collective-permute-done((bf16[2,32,512]{1,2,0:T(8,128)(2,1)S(1)}, bf16[2,32,512]{1,2,0:T(8,128)(2,1)S(1)}, u32[]{:S(2)}, u32[]{:S(2)}) %collective-permute-start.1) | collective-permute-done | bytes 65568 | tf_op jit(solution)/shard_map/while/body/eval_jaxpr/ppermute | solution.py:15
  66.9 1.9 collective-permute-start
  68.9 2.4 collective-permute-start.1
  71.3 2.5 collective-permute-done
  74.0 4.7 %collective-permute-done.1 = bf16[2,32,512]{1,2,0:T(8,128)(2,1)S(1)} collective-permute-done((bf16[2,32,512]{1,2,0:T(8,128)(2,1)S(1)}, bf16[2,32,512]{1,2,0:T(8,128)(2,1)S(1)}, u32[]{:S(2)}, u32[]{:S(2)}) %collective-permute-start.1) | collective-permute-done | bytes 65568 | tf_op jit(solution)/shard_map/while/body/eval_jaxpr/ppermute | solution.py:15
  79.4 1.9 collective-permute-start
  81.4 2.4 collective-permute-start.1
  83.8 2.5 collective-permute-done
  86.5 6.0 %collective-permute-done.1 = bf16[2,32,512]{1,2,0:T(8,128)(2,1)S(1)} collective-permute-done((bf16[2,32,512]{1,2,0:T(8,128)(2,1)S(1)}, bf16[2,32,512]{1,2,0:T(8,128)(2,1)S(1)}, u32[]{:S(2)}, u32[]{:S(2)}) %collective-permute-start.1) | collective-permute-done | bytes 65568 | tf_op jit(solution)/shard_map/while/body/eval_jaxpr/ppermute | solution.py:15
  93.2 1.9 collective-permute-start
  95.2 2.4 collective-permute-start.1
  97.6 2.5 collective-permute-done
  100.3 7.3 %collective-permute-done.1 = bf16[2,32,512]{1,2,0:T(8,128)(2,1)S(1)} collective-permute-done((bf16[2,32,512]{1,2,0:T(8,128)(2,1)S(1)}, bf16[2,32,512]{1,2,0:T(8,128)(2,1)S(1)}, u32[]{:S(2)}, u32[]{:S(2)}) %collective-permute-start.1) | collective-permute-done | bytes 65568 | tf_op jit(solution)/shard_map/while/body/eval_jaxpr/ppermute | solution.py:15
  108.3 1.9 collective-permute-start
  110.3 2.4 collective-permute-start.1
  112.7 2.5 collective-permute-done
  115.4 7.4 %collective-permute-done.1 = bf16[2,32,512]{1,2,0:T(8,128)(2,1)S(1)} collective-permute-done((bf16[2,32,512]{1,2,0:T(8,128)(2,1)S(1)}, bf16[2,32,512]{1,2,0:T(8,128)(2,1)S(1)}, u32[]{:S(2)}, u32[]{:S(2)}) %collective-permute-start.1) | collective-permute-done | bytes 65568 | tf_op jit(solution)/shard_map/while/body/eval_jaxpr/ppermute | solution.py:15
  123.5 1.9 collective-permute-start
  125.4 2.4 collective-permute-start.1
  127.8 2.5 collective-permute-done
  130.5 7.4 %collective-permute-done.1 = bf16[2,32,512]{1,2,0:T(8,128)(2,1)S(1)} collective-permute-done((bf16[2,32,512]{1,2,0:T(8,128)(2,1)S(1)}, bf16[2,32,512]{1,2,0:T(8,128)(2,1)S(1)}, u32[]{:S(2)}, u32[]{:S(2)}) %collective-permute-start.1) | collective-permute-done | bytes 65568 | tf_op jit(solution)/shard_map/while/body/eval_jaxpr/ppermute | solution.py:15
  138.9 138.1 %while.21 = (s32[]{:T(128)}, bf16[2,256,512]{1,2,0:T(8,128)(2,1)S(1)}, bf16[32,256]{1,0:T(8,128)(2,1)S(1)}, bf16[32,256]{1,0:T(8,128)(2,1)S(1)}, f32[2,256,512]{...) while((s32[]{:T(128)}, bf16[2,256,512]{1,2,0:T(8,128)(2,1)S(1)}, ...), condition=%wide.region_3.0_spmd, body=%wide.region_2.0_spmd.sunk | while | flops 169213952 | bytes 4230837 | solution.py:89
  139.2 1.9 collective-permute-start.2
  141.4 2.4 collective-permute-start.3
  145.7 7.6 %collective-permute-done.3 = bf16[2,32,512]{1,2,0:T(8,128)(2,1)S(1)} collective-permute-done((bf16[2,32,512]{1,2,0:T(8,128)(2,1)S(1)}, bf16[2,32,512]{1,2,0:T(8,128)(2,1)S(1)}, u32[]{:S(2)}, u32[]{:S(2)}) %collective-permute-start.3) | collective-permute-done | bytes 65568 | tf_op jit(solution)/shard_map/while/body/eval_jaxpr/ppermute | solution.py:15
  154.0 1.9 collective-permute-start.2
  156.2 2.4 collective-permute-start.3
  160.6 8.1 %collective-permute-done.3 = bf16[2,32,512]{1,2,0:T(8,128)(2,1)S(1)} collective-permute-done((bf16[2,32,512]{1,2,0:T(8,128)(2,1)S(1)}, bf16[2,32,512]{1,2,0:T(8,128)(2,1)S(1)}, u32[]{:S(2)}, u32[]{:S(2)}) %collective-permute-start.3) | collective-permute-done | bytes 65568 | tf_op jit(solution)/shard_map/while/body/eval_jaxpr/ppermute | solution.py:15
  169.3 1.9 collective-permute-start.2
  171.5 2.4 collective-permute-start.3
  175.9 8.1 %collective-permute-done.3 = bf16[2,32,512]{1,2,0:T(8,128)(2,1)S(1)} collective-permute-done((bf16[2,32,512]{1,2,0:T(8,128)(2,1)S(1)}, bf16[2,32,512]{1,2,0:T(8,128)(2,1)S(1)}, u32[]{:S(2)}, u32[]{:S(2)}) %collective-permute-start.3) | collective-permute-done | bytes 65568 | tf_op jit(solution)/shard_map/while/body/eval_jaxpr/ppermute | solution.py:15
  184.7 1.9 collective-permute-start.2
  186.9 2.4 collective-permute-start.3
  191.3 8.2 %collective-permute-done.3 = bf16[2,32,512]{1,2,0:T(8,128)(2,1)S(1)} collective-permute-done((bf16[2,32,512]{1,2,0:T(8,128)(2,1)S(1)}, bf16[2,32,512]{1,2,0:T(8,128)(2,1)S(1)}, u32[]{:S(2)}, u32[]{:S(2)}) %collective-permute-start.3) | collective-permute-done | bytes 65568 | tf_op jit(solution)/shard_map/while/body/eval_jaxpr/ppermute | solution.py:15
  200.1 1.9 collective-permute-start.2
  202.3 2.4 collective-permute-start.3
  206.7 8.2 %collective-permute-done.3 = bf16[2,32,512]{1,2,0:T(8,128)(2,1)S(1)} collective-permute-done((bf16[2,32,512]{1,2,0:T(8,128)(2,1)S(1)}, bf16[2,32,512]{1,2,0:T(8,128)(2,1)S(1)}, u32[]{:S(2)}, u32[]{:S(2)}) %collective-permute-start.3) | collective-permute-done | bytes 65568 | tf_op jit(solution)/shard_map/while/body/eval_jaxpr/ppermute | solution.py:15
  215.6 1.9 collective-permute-start.2
  217.8 2.4 collective-permute-start.3
  222.1 8.2 %collective-permute-done.3 = bf16[2,32,512]{1,2,0:T(8,128)(2,1)S(1)} collective-permute-done((bf16[2,32,512]{1,2,0:T(8,128)(2,1)S(1)}, bf16[2,32,512]{1,2,0:T(8,128)(2,1)S(1)}, u32[]{:S(2)}, u32[]{:S(2)}) %collective-permute-start.3) | collective-permute-done | bytes 65568 | tf_op jit(solution)/shard_map/while/body/eval_jaxpr/ppermute | solution.py:15
  231.0 1.9 collective-permute-start.2
  233.2 2.4 collective-permute-start.3
  237.6 8.2 %collective-permute-done.3 = bf16[2,32,512]{1,2,0:T(8,128)(2,1)S(1)} collective-permute-done((bf16[2,32,512]{1,2,0:T(8,128)(2,1)S(1)}, bf16[2,32,512]{1,2,0:T(8,128)(2,1)S(1)}, u32[]{:S(2)}, u32[]{:S(2)}) %collective-permute-start.3) | collective-permute-done | bytes 65568 | tf_op jit(solution)/shard_map/while/body/eval_jaxpr/ppermute | solution.py:15
  248.6 2.4 collective-permute-start.3
  253.0 8.2 %collective-permute-done.3 = bf16[2,32,512]{1,2,0:T(8,128)(2,1)S(1)} collective-permute-done((bf16[2,32,512]{1,2,0:T(8,128)(2,1)S(1)}, bf16[2,32,512]{1,2,0:T(8,128)(2,1)S(1)}, u32[]{:S(2)}, u32[]{:S(2)}) %collective-permute-start.3) | collective-permute-done | bytes 65568 | tf_op jit(solution)/shard_map/while/body/eval_jaxpr/ppermute | solution.py:15
  261.8 1.9 collective-permute-start.2
  264.0 2.4 collective-permute-start.3
  268.4 8.2 %collective-permute-done.3 = bf16[2,32,512]{1,2,0:T(8,128)(2,1)S(1)} collective-permute-done((bf16[2,32,512]{1,2,0:T(8,128)(2,1)S(1)}, bf16[2,32,512]{1,2,0:T(8,128)(2,1)S(1)}, u32[]{:S(2)}, u32[]{:S(2)}) %collective-permute-start.3) | collective-permute-done | bytes 65568 | tf_op jit(solution)/shard_map/while/body/eval_jaxpr/ppermute | solution.py:15
  278.0 170.3 %all-reduce.2.cloned.1.call-done = f32[256,256]{1,0:T(8,128)} async-done(((f32[256,256]{1,0:T(8,128)}), f32[256,256]{1,0:T(8,128)}) %all-reduce.2.cloned.1.call-update) | async-done | bytes 262160 | tf_op jit(solution)/shard_map/psum | solution.py:92
  (123 shorter events, 42.0 us)
Async XLA Ops:
  6.5 1.3 copy-start.1
  6.5 1.3 copy-start
  6.5 441.8 %all-reduce.2.cloned.1.call-start = ((), (), s32[]{:S(2)}) async-start(), calls=%async_computation | async-start | bytes 524288 | tf_op jit(solution)/shard_map/psum | solution.py:92
  8.2 1.6 copy-start.4
  8.2 1.6 copy-start.3
  8.4 1.4 copy-start.2
  10.0 5.8 %collective-permute-start = (bf16[2,32,512]{1,2,0:T(8,128)(2,1)S(1)}, bf16[2,32,512]{1,2,0:T(8,128)(2,1)S(1)}, u32[]{:S(2)}, u32[]{:S(2)}) collective-permute-start(bf16[2,32,512]{1,2,0:T(8,128)(2,1)S(1)} %get-tuple-element.173), channel_id=1, source_target_pairs={{1,0},{2,1},{3,2},{4,3},{5,4},{6,5},{7,6},{8,7},{9,8},{10,9},{11,1... | collective-permute-start | bytes 196616 | tf_op jit(solution)/shard_map/while/body/eval_jaxpr/ppermute | solution.py:18
  11.9 12.3 %collective-permute-start.1 = (bf16[2,32,512]{1,2,0:T(8,128)(2,1)S(1)}, bf16[2,32,512]{1,2,0:T(8,128)(2,1)S(1)}, u32[]{:S(2)}, u32[]{:S(2)}) collective-permute-start(bf16[2,32,512]{1,2,0:T(8,128)(2,1)S(1)} %get-tuple-element.174), channel_id=1, source_target_pairs={{0,1},{1,2},{2,3},{3,4},{4,5},{5,6},{6,7},{7,8},{8,9},{9,10},{10,1... | collective-permute-start | bytes 196616 | tf_op jit(solution)/shard_map/while/body/eval_jaxpr/ppermute | solution.py:15
  24.9 8.3 %collective-permute-start = (bf16[2,32,512]{1,2,0:T(8,128)(2,1)S(1)}, bf16[2,32,512]{1,2,0:T(8,128)(2,1)S(1)}, u32[]{:S(2)}, u32[]{:S(2)}) collective-permute-start(bf16[2,32,512]{1,2,0:T(8,128)(2,1)S(1)} %get-tuple-element.173), channel_id=1, source_target_pairs={{1,0},{2,1},{3,2},{4,3},{5,4},{6,5},{7,6},{8,7},{9,8},{10,9},{11,1... | collective-permute-start | bytes 196616 | tf_op jit(solution)/shard_map/while/body/eval_jaxpr/ppermute | solution.py:18
  27.5 13.9 %collective-permute-start.1 = (bf16[2,32,512]{1,2,0:T(8,128)(2,1)S(1)}, bf16[2,32,512]{1,2,0:T(8,128)(2,1)S(1)}, u32[]{:S(2)}, u32[]{:S(2)}) collective-permute-start(bf16[2,32,512]{1,2,0:T(8,128)(2,1)S(1)} %get-tuple-element.174), channel_id=1, source_target_pairs={{0,1},{1,2},{2,3},{3,4},{4,5},{5,6},{6,7},{7,8},{8,9},{9,10},{10,1... | collective-permute-start | bytes 196616 | tf_op jit(solution)/shard_map/while/body/eval_jaxpr/ppermute | solution.py:15
  42.1 6.8 %collective-permute-start = (bf16[2,32,512]{1,2,0:T(8,128)(2,1)S(1)}, bf16[2,32,512]{1,2,0:T(8,128)(2,1)S(1)}, u32[]{:S(2)}, u32[]{:S(2)}) collective-permute-start(bf16[2,32,512]{1,2,0:T(8,128)(2,1)S(1)} %get-tuple-element.173), channel_id=1, source_target_pairs={{1,0},{2,1},{3,2},{4,3},{5,4},{6,5},{7,6},{8,7},{9,8},{10,9},{11,1... | collective-permute-start | bytes 196616 | tf_op jit(solution)/shard_map/while/body/eval_jaxpr/ppermute | solution.py:18
  44.0 9.8 %collective-permute-start.1 = (bf16[2,32,512]{1,2,0:T(8,128)(2,1)S(1)}, bf16[2,32,512]{1,2,0:T(8,128)(2,1)S(1)}, u32[]{:S(2)}, u32[]{:S(2)}) collective-permute-start(bf16[2,32,512]{1,2,0:T(8,128)(2,1)S(1)} %get-tuple-element.174), channel_id=1, source_target_pairs={{0,1},{1,2},{2,3},{3,4},{4,5},{5,6},{6,7},{7,8},{8,9},{9,10},{10,1... | collective-permute-start | bytes 196616 | tf_op jit(solution)/shard_map/while/body/eval_jaxpr/ppermute | solution.py:15
  54.5 6.8 %collective-permute-start = (bf16[2,32,512]{1,2,0:T(8,128)(2,1)S(1)}, bf16[2,32,512]{1,2,0:T(8,128)(2,1)S(1)}, u32[]{:S(2)}, u32[]{:S(2)}) collective-permute-start(bf16[2,32,512]{1,2,0:T(8,128)(2,1)S(1)} %get-tuple-element.173), channel_id=1, source_target_pairs={{1,0},{2,1},{3,2},{4,3},{5,4},{6,5},{7,6},{8,7},{9,8},{10,9},{11,1... | collective-permute-start | bytes 196616 | tf_op jit(solution)/shard_map/while/body/eval_jaxpr/ppermute | solution.py:18
  56.5 9.8 %collective-permute-start.1 = (bf16[2,32,512]{1,2,0:T(8,128)(2,1)S(1)}, bf16[2,32,512]{1,2,0:T(8,128)(2,1)S(1)}, u32[]{:S(2)}, u32[]{:S(2)}) collective-permute-start(bf16[2,32,512]{1,2,0:T(8,128)(2,1)S(1)} %get-tuple-element.174), channel_id=1, source_target_pairs={{0,1},{1,2},{2,3},{3,4},{4,5},{5,6},{6,7},{7,8},{8,9},{9,10},{10,1... | collective-permute-start | bytes 196616 | tf_op jit(solution)/shard_map/while/body/eval_jaxpr/ppermute | solution.py:15
  66.9 6.8 %collective-permute-start = (bf16[2,32,512]{1,2,0:T(8,128)(2,1)S(1)}, bf16[2,32,512]{1,2,0:T(8,128)(2,1)S(1)}, u32[]{:S(2)}, u32[]{:S(2)}) collective-permute-start(bf16[2,32,512]{1,2,0:T(8,128)(2,1)S(1)} %get-tuple-element.173), channel_id=1, source_target_pairs={{1,0},{2,1},{3,2},{4,3},{5,4},{6,5},{7,6},{8,7},{9,8},{10,9},{11,1... | collective-permute-start | bytes 196616 | tf_op jit(solution)/shard_map/while/body/eval_jaxpr/ppermute | solution.py:18
  68.9 9.9 %collective-permute-start.1 = (bf16[2,32,512]{1,2,0:T(8,128)(2,1)S(1)}, bf16[2,32,512]{1,2,0:T(8,128)(2,1)S(1)}, u32[]{:S(2)}, u32[]{:S(2)}) collective-permute-start(bf16[2,32,512]{1,2,0:T(8,128)(2,1)S(1)} %get-tuple-element.174), channel_id=1, source_target_pairs={{0,1},{1,2},{2,3},{3,4},{4,5},{5,6},{6,7},{7,8},{8,9},{9,10},{10,1... | collective-permute-start | bytes 196616 | tf_op jit(solution)/shard_map/while/body/eval_jaxpr/ppermute | solution.py:15
  79.4 6.8 %collective-permute-start = (bf16[2,32,512]{1,2,0:T(8,128)(2,1)S(1)}, bf16[2,32,512]{1,2,0:T(8,128)(2,1)S(1)}, u32[]{:S(2)}, u32[]{:S(2)}) collective-permute-start(bf16[2,32,512]{1,2,0:T(8,128)(2,1)S(1)} %get-tuple-element.173), channel_id=1, source_target_pairs={{1,0},{2,1},{3,2},{4,3},{5,4},{6,5},{7,6},{8,7},{9,8},{10,9},{11,1... | collective-permute-start | bytes 196616 | tf_op jit(solution)/shard_map/while/body/eval_jaxpr/ppermute | solution.py:18
  81.4 11.2 %collective-permute-start.1 = (bf16[2,32,512]{1,2,0:T(8,128)(2,1)S(1)}, bf16[2,32,512]{1,2,0:T(8,128)(2,1)S(1)}, u32[]{:S(2)}, u32[]{:S(2)}) collective-permute-start(bf16[2,32,512]{1,2,0:T(8,128)(2,1)S(1)} %get-tuple-element.174), channel_id=1, source_target_pairs={{0,1},{1,2},{2,3},{3,4},{4,5},{5,6},{6,7},{7,8},{8,9},{9,10},{10,1... | collective-permute-start | bytes 196616 | tf_op jit(solution)/shard_map/while/body/eval_jaxpr/ppermute | solution.py:15
  93.2 6.8 %collective-permute-start = (bf16[2,32,512]{1,2,0:T(8,128)(2,1)S(1)}, bf16[2,32,512]{1,2,0:T(8,128)(2,1)S(1)}, u32[]{:S(2)}, u32[]{:S(2)}) collective-permute-start(bf16[2,32,512]{1,2,0:T(8,128)(2,1)S(1)} %get-tuple-element.173), channel_id=1, source_target_pairs={{1,0},{2,1},{3,2},{4,3},{5,4},{6,5},{7,6},{8,7},{9,8},{10,9},{11,1... | collective-permute-start | bytes 196616 | tf_op jit(solution)/shard_map/while/body/eval_jaxpr/ppermute | solution.py:18
  95.2 12.5 %collective-permute-start.1 = (bf16[2,32,512]{1,2,0:T(8,128)(2,1)S(1)}, bf16[2,32,512]{1,2,0:T(8,128)(2,1)S(1)}, u32[]{:S(2)}, u32[]{:S(2)}) collective-permute-start(bf16[2,32,512]{1,2,0:T(8,128)(2,1)S(1)} %get-tuple-element.174), channel_id=1, source_target_pairs={{0,1},{1,2},{2,3},{3,4},{4,5},{5,6},{6,7},{7,8},{8,9},{9,10},{10,1... | collective-permute-start | bytes 196616 | tf_op jit(solution)/shard_map/while/body/eval_jaxpr/ppermute | solution.py:15
  108.3 6.8 %collective-permute-start = (bf16[2,32,512]{1,2,0:T(8,128)(2,1)S(1)}, bf16[2,32,512]{1,2,0:T(8,128)(2,1)S(1)}, u32[]{:S(2)}, u32[]{:S(2)}) collective-permute-start(bf16[2,32,512]{1,2,0:T(8,128)(2,1)S(1)} %get-tuple-element.173), channel_id=1, source_target_pairs={{1,0},{2,1},{3,2},{4,3},{5,4},{6,5},{7,6},{8,7},{9,8},{10,9},{11,1... | collective-permute-start | bytes 196616 | tf_op jit(solution)/shard_map/while/body/eval_jaxpr/ppermute | solution.py:18
  110.3 12.5 %collective-permute-start.1 = (bf16[2,32,512]{1,2,0:T(8,128)(2,1)S(1)}, bf16[2,32,512]{1,2,0:T(8,128)(2,1)S(1)}, u32[]{:S(2)}, u32[]{:S(2)}) collective-permute-start(bf16[2,32,512]{1,2,0:T(8,128)(2,1)S(1)} %get-tuple-element.174), channel_id=1, source_target_pairs={{0,1},{1,2},{2,3},{3,4},{4,5},{5,6},{6,7},{7,8},{8,9},{9,10},{10,1... | collective-permute-start | bytes 196616 | tf_op jit(solution)/shard_map/while/body/eval_jaxpr/ppermute | solution.py:15
  123.5 6.8 %collective-permute-start = (bf16[2,32,512]{1,2,0:T(8,128)(2,1)S(1)}, bf16[2,32,512]{1,2,0:T(8,128)(2,1)S(1)}, u32[]{:S(2)}, u32[]{:S(2)}) collective-permute-start(bf16[2,32,512]{1,2,0:T(8,128)(2,1)S(1)} %get-tuple-element.173), channel_id=1, source_target_pairs={{1,0},{2,1},{3,2},{4,3},{5,4},{6,5},{7,6},{8,7},{9,8},{10,9},{11,1... | collective-permute-start | bytes 196616 | tf_op jit(solution)/shard_map/while/body/eval_jaxpr/ppermute | solution.py:18
  125.4 12.5 %collective-permute-start.1 = (bf16[2,32,512]{1,2,0:T(8,128)(2,1)S(1)}, bf16[2,32,512]{1,2,0:T(8,128)(2,1)S(1)}, u32[]{:S(2)}, u32[]{:S(2)}) collective-permute-start(bf16[2,32,512]{1,2,0:T(8,128)(2,1)S(1)} %get-tuple-element.174), channel_id=1, source_target_pairs={{0,1},{1,2},{2,3},{3,4},{4,5},{5,6},{6,7},{7,8},{8,9},{9,10},{10,1... | collective-permute-start | bytes 196616 | tf_op jit(solution)/shard_map/while/body/eval_jaxpr/ppermute | solution.py:15
  139.2 6.5 %collective-permute-start.2 = (bf16[2,32,512]{1,2,0:T(8,128)(2,1)S(1)}, bf16[2,32,512]{1,2,0:T(8,128)(2,1)S(1)}, u32[]{:S(2)}, u32[]{:S(2)}) collective-permute-start(bf16[2,32,512]{1,2,0:T(8,128)(2,1)S(1)} %fusion.64), channel_id=1, source_target_pairs={{1,0},{2,1},{3,2},{4,3},{5,4},{6,5},{7,6},{8,7},{9,8},{10,9},{11,1... | collective-permute-start | bytes 196616 | tf_op jit(solution)/shard_map/while/body/eval_jaxpr/ppermute | solution.py:18
  141.4 12.0 %collective-permute-start.3 = (bf16[2,32,512]{1,2,0:T(8,128)(2,1)S(1)}, bf16[2,32,512]{1,2,0:T(8,128)(2,1)S(1)}, u32[]{:S(2)}, u32[]{:S(2)}) collective-permute-start(bf16[2,32,512]{1,2,0:T(8,128)(2,1)S(1)} %fusion.65), channel_id=1, source_target_pairs={{0,1},{1,2},{2,3},{3,4},{4,5},{5,6},{6,7},{7,8},{8,9},{9,10},{10,1... | collective-permute-start | bytes 196616 | tf_op jit(solution)/shard_map/while/body/eval_jaxpr/ppermute | solution.py:15
  154.0 6.5 %collective-permute-start.2 = (bf16[2,32,512]{1,2,0:T(8,128)(2,1)S(1)}, bf16[2,32,512]{1,2,0:T(8,128)(2,1)S(1)}, u32[]{:S(2)}, u32[]{:S(2)}) collective-permute-start(bf16[2,32,512]{1,2,0:T(8,128)(2,1)S(1)} %fusion.64), channel_id=1, source_target_pairs={{1,0},{2,1},{3,2},{4,3},{5,4},{6,5},{7,6},{8,7},{9,8},{10,9},{11,1... | collective-permute-start | bytes 196616 | tf_op jit(solution)/shard_map/while/body/eval_jaxpr/ppermute | solution.py:18
  156.2 12.4 %collective-permute-start.3 = (bf16[2,32,512]{1,2,0:T(8,128)(2,1)S(1)}, bf16[2,32,512]{1,2,0:T(8,128)(2,1)S(1)}, u32[]{:S(2)}, u32[]{:S(2)}) collective-permute-start(bf16[2,32,512]{1,2,0:T(8,128)(2,1)S(1)} %fusion.65), channel_id=1, source_target_pairs={{0,1},{1,2},{2,3},{3,4},{4,5},{5,6},{6,7},{7,8},{8,9},{9,10},{10,1... | collective-permute-start | bytes 196616 | tf_op jit(solution)/shard_map/while/body/eval_jaxpr/ppermute | solution.py:15
  169.3 6.5 %collective-permute-start.2 = (bf16[2,32,512]{1,2,0:T(8,128)(2,1)S(1)}, bf16[2,32,512]{1,2,0:T(8,128)(2,1)S(1)}, u32[]{:S(2)}, u32[]{:S(2)}) collective-permute-start(bf16[2,32,512]{1,2,0:T(8,128)(2,1)S(1)} %fusion.64), channel_id=1, source_target_pairs={{1,0},{2,1},{3,2},{4,3},{5,4},{6,5},{7,6},{8,7},{9,8},{10,9},{11,1... | collective-permute-start | bytes 196616 | tf_op jit(solution)/shard_map/while/body/eval_jaxpr/ppermute | solution.py:18
  171.5 12.5 %collective-permute-start.3 = (bf16[2,32,512]{1,2,0:T(8,128)(2,1)S(1)}, bf16[2,32,512]{1,2,0:T(8,128)(2,1)S(1)}, u32[]{:S(2)}, u32[]{:S(2)}) collective-permute-start(bf16[2,32,512]{1,2,0:T(8,128)(2,1)S(1)} %fusion.65), channel_id=1, source_target_pairs={{0,1},{1,2},{2,3},{3,4},{4,5},{5,6},{6,7},{7,8},{8,9},{9,10},{10,1... | collective-permute-start | bytes 196616 | tf_op jit(solution)/shard_map/while/body/eval_jaxpr/ppermute | solution.py:15
  184.7 6.5 %collective-permute-start.2 = (bf16[2,32,512]{1,2,0:T(8,128)(2,1)S(1)}, bf16[2,32,512]{1,2,0:T(8,128)(2,1)S(1)}, u32[]{:S(2)}, u32[]{:S(2)}) collective-permute-start(bf16[2,32,512]{1,2,0:T(8,128)(2,1)S(1)} %fusion.64), channel_id=1, source_target_pairs={{1,0},{2,1},{3,2},{4,3},{5,4},{6,5},{7,6},{8,7},{9,8},{10,9},{11,1... | collective-permute-start | bytes 196616 | tf_op jit(solution)/shard_map/while/body/eval_jaxpr/ppermute | solution.py:18
  186.9 12.5 %collective-permute-start.3 = (bf16[2,32,512]{1,2,0:T(8,128)(2,1)S(1)}, bf16[2,32,512]{1,2,0:T(8,128)(2,1)S(1)}, u32[]{:S(2)}, u32[]{:S(2)}) collective-permute-start(bf16[2,32,512]{1,2,0:T(8,128)(2,1)S(1)} %fusion.65), channel_id=1, source_target_pairs={{0,1},{1,2},{2,3},{3,4},{4,5},{5,6},{6,7},{7,8},{8,9},{9,10},{10,1... | collective-permute-start | bytes 196616 | tf_op jit(solution)/shard_map/while/body/eval_jaxpr/ppermute | solution.py:15
  200.1 6.5 %collective-permute-start.2 = (bf16[2,32,512]{1,2,0:T(8,128)(2,1)S(1)}, bf16[2,32,512]{1,2,0:T(8,128)(2,1)S(1)}, u32[]{:S(2)}, u32[]{:S(2)}) collective-permute-start(bf16[2,32,512]{1,2,0:T(8,128)(2,1)S(1)} %fusion.64), channel_id=1, source_target_pairs={{1,0},{2,1},{3,2},{4,3},{5,4},{6,5},{7,6},{8,7},{9,8},{10,9},{11,1... | collective-permute-start | bytes 196616 | tf_op jit(solution)/shard_map/while/body/eval_jaxpr/ppermute | solution.py:18
  202.3 12.5 %collective-permute-start.3 = (bf16[2,32,512]{1,2,0:T(8,128)(2,1)S(1)}, bf16[2,32,512]{1,2,0:T(8,128)(2,1)S(1)}, u32[]{:S(2)}, u32[]{:S(2)}) collective-permute-start(bf16[2,32,512]{1,2,0:T(8,128)(2,1)S(1)} %fusion.65), channel_id=1, source_target_pairs={{0,1},{1,2},{2,3},{3,4},{4,5},{5,6},{6,7},{7,8},{8,9},{9,10},{10,1... | collective-permute-start | bytes 196616 | tf_op jit(solution)/shard_map/while/body/eval_jaxpr/ppermute | solution.py:15
  215.6 6.5 %collective-permute-start.2 = (bf16[2,32,512]{1,2,0:T(8,128)(2,1)S(1)}, bf16[2,32,512]{1,2,0:T(8,128)(2,1)S(1)}, u32[]{:S(2)}, u32[]{:S(2)}) collective-permute-start(bf16[2,32,512]{1,2,0:T(8,128)(2,1)S(1)} %fusion.64), channel_id=1, source_target_pairs={{1,0},{2,1},{3,2},{4,3},{5,4},{6,5},{7,6},{8,7},{9,8},{10,9},{11,1... | collective-permute-start | bytes 196616 | tf_op jit(solution)/shard_map/while/body/eval_jaxpr/ppermute | solution.py:18
  217.8 12.5 %collective-permute-start.3 = (bf16[2,32,512]{1,2,0:T(8,128)(2,1)S(1)}, bf16[2,32,512]{1,2,0:T(8,128)(2,1)S(1)}, u32[]{:S(2)}, u32[]{:S(2)}) collective-permute-start(bf16[2,32,512]{1,2,0:T(8,128)(2,1)S(1)} %fusion.65), channel_id=1, source_target_pairs={{0,1},{1,2},{2,3},{3,4},{4,5},{5,6},{6,7},{7,8},{8,9},{9,10},{10,1... | collective-permute-start | bytes 196616 | tf_op jit(solution)/shard_map/while/body/eval_jaxpr/ppermute | solution.py:15
  231.0 6.5 %collective-permute-start.2 = (bf16[2,32,512]{1,2,0:T(8,128)(2,1)S(1)}, bf16[2,32,512]{1,2,0:T(8,128)(2,1)S(1)}, u32[]{:S(2)}, u32[]{:S(2)}) collective-permute-start(bf16[2,32,512]{1,2,0:T(8,128)(2,1)S(1)} %fusion.64), channel_id=1, source_target_pairs={{1,0},{2,1},{3,2},{4,3},{5,4},{6,5},{7,6},{8,7},{9,8},{10,9},{11,1... | collective-permute-start | bytes 196616 | tf_op jit(solution)/shard_map/while/body/eval_jaxpr/ppermute | solution.py:18
  233.2 12.5 %collective-permute-start.3 = (bf16[2,32,512]{1,2,0:T(8,128)(2,1)S(1)}, bf16[2,32,512]{1,2,0:T(8,128)(2,1)S(1)}, u32[]{:S(2)}, u32[]{:S(2)}) collective-permute-start(bf16[2,32,512]{1,2,0:T(8,128)(2,1)S(1)} %fusion.65), channel_id=1, source_target_pairs={{0,1},{1,2},{2,3},{3,4},{4,5},{5,6},{6,7},{7,8},{8,9},{9,10},{10,1... | collective-permute-start | bytes 196616 | tf_op jit(solution)/shard_map/while/body/eval_jaxpr/ppermute | solution.py:15
  246.4 6.5 %collective-permute-start.2 = (bf16[2,32,512]{1,2,0:T(8,128)(2,1)S(1)}, bf16[2,32,512]{1,2,0:T(8,128)(2,1)S(1)}, u32[]{:S(2)}, u32[]{:S(2)}) collective-permute-start(bf16[2,32,512]{1,2,0:T(8,128)(2,1)S(1)} %fusion.64), channel_id=1, source_target_pairs={{1,0},{2,1},{3,2},{4,3},{5,4},{6,5},{7,6},{8,7},{9,8},{10,9},{11,1... | collective-permute-start | bytes 196616 | tf_op jit(solution)/shard_map/while/body/eval_jaxpr/ppermute | solution.py:18
  248.6 12.5 %collective-permute-start.3 = (bf16[2,32,512]{1,2,0:T(8,128)(2,1)S(1)}, bf16[2,32,512]{1,2,0:T(8,128)(2,1)S(1)}, u32[]{:S(2)}, u32[]{:S(2)}) collective-permute-start(bf16[2,32,512]{1,2,0:T(8,128)(2,1)S(1)} %fusion.65), channel_id=1, source_target_pairs={{0,1},{1,2},{2,3},{3,4},{4,5},{5,6},{6,7},{7,8},{8,9},{9,10},{10,1... | collective-permute-start | bytes 196616 | tf_op jit(solution)/shard_map/while/body/eval_jaxpr/ppermute | solution.py:15
  261.8 6.5 %collective-permute-start.2 = (bf16[2,32,512]{1,2,0:T(8,128)(2,1)S(1)}, bf16[2,32,512]{1,2,0:T(8,128)(2,1)S(1)}, u32[]{:S(2)}, u32[]{:S(2)}) collective-permute-start(bf16[2,32,512]{1,2,0:T(8,128)(2,1)S(1)} %fusion.64), channel_id=1, source_target_pairs={{1,0},{2,1},{3,2},{4,3},{5,4},{6,5},{7,6},{8,7},{9,8},{10,9},{11,1... | collective-permute-start | bytes 196616 | tf_op jit(solution)/shard_map/while/body/eval_jaxpr/ppermute | solution.py:18
  264.0 12.5 %collective-permute-start.3 = (bf16[2,32,512]{1,2,0:T(8,128)(2,1)S(1)}, bf16[2,32,512]{1,2,0:T(8,128)(2,1)S(1)}, u32[]{:S(2)}, u32[]{:S(2)}) collective-permute-start(bf16[2,32,512]{1,2,0:T(8,128)(2,1)S(1)} %fusion.65), channel_id=1, source_target_pairs={{0,1},{1,2},{2,3},{3,4},{4,5},{5,6},{6,7},{7,8},{8,9},{9,10},{10,1... | collective-permute-start | bytes 196616 | tf_op jit(solution)/shard_map/while/body/eval_jaxpr/ppermute | solution.py:15
Sparse Core Ops, SparseCore 0:
  278.2 170.1 all-reduce.1
where the time goes:
time: 459 us; the launch traced here: 457 us
  waiting for transfers between devices  340 us (74%)
  starting transfers between devices  78.2 us (17%)
  matrix products  16.6 us (4%)
  between operations  14.8 us (3%)
  local copies, waits for them, and re-layouts  4.8 us (1%)
    psum x1, waiting for transfers between devices, body(): full = lax.psum(product * (-1.0 / modes), 'energy')  170 us
    ppermute x18, waiting for transfers between devices, with_halo(): lax.ppermute(lax.slice_in_dim(block, block.shape[dim] - width, None, axis...  131 us
    ppermute x18, starting transfers between devices, with_halo(): lax.ppermute(lax.slice_in_dim(block, block.shape[dim] - width, None, axis...  42.9 us
    ppermute x18, waiting for transfers between devices, with_halo(): lax.ppermute(lax.slice_in_dim(block, 0, width, axis=dim), axis, backward)  38.8 us
    ppermute x18, starting transfers between devices, with_halo(): lax.ppermute(lax.slice_in_dim(block, 0, width, axis=dim), axis, backward)  35.3 us
  transfers between devices with their start and end apart: 37, of which 37 were waited for; matrix products, arithmetic and copies ran while one was open for 1% of the time, Pallas kernels for 0%

commit v1 on v0

v1 whole, which is shorter than its diff:
```python
import jax
import jax.numpy as jnp
from jax import lax
from jax.experimental import pallas as pl
from jax.experimental.pallas import tpu as pltpu
from jax.sharding import PartitionSpec as P

SWEEPS = 10
LANES = 128
F32 = jnp.float32
BF16 = jnp.bfloat16


def mm(a, b):
    return jnp.dot(a, b, preferred_element_type=F32)


def mm_nt(a, b):
    return lax.dot_general(a, b, (((1,), (1,)), ((), ())), preferred_element_type=F32)


def collector_row(low_ref, high_ref, shape, dim):
    at = lax.broadcasted_iota(jnp.int32, shape, dim)
    return (at >= low_ref[0]) & (at < high_ref[0])


def prepare(
    w_ref, low_ref, high_ref, p_hbm, b_hbm, l_hbm, r_hbm, o_ref, p_ref, b_ref, c_ref, sems
):
    count, block, modes = b_ref.shape
    edge = l_hbm.shape[0]
    copies = [
        pltpu.make_async_copy(l_hbm, c_ref.at[pl.ds(0, edge)], sems.at[0]),
        pltpu.make_async_copy(r_hbm, c_ref.at[pl.ds(edge, edge)], sems.at[1]),
        pltpu.make_async_copy(p_hbm, p_ref, sems.at[2]),
        pltpu.make_async_copy(b_hbm, b_ref, sems.at[3]),
    ]
    for copy in copies:
        copy.start()
    for copy in copies[:3]:
        copy.wait()
    couple = c_ref[...]
    inside = collector_row(low_ref, high_ref, (1, block), 1)
    chunk = o_ref.shape[1] - 2 * edge
    each = modes // chunk
    stacks = []
    for e in range(count):
        inverse = p_ref[e]
        rim = jnp.concatenate([inverse[block - edge :], inverse[:edge]], axis=0)
        u = mm_nt(couple, inverse)
        weighted = jnp.where(inside, u * (2.0 * w_ref[e]), 0.0).astype(BF16)
        step = mm_nt(couple, rim)
        middle = mm_nt(weighted, u.astype(BF16))
        exact = jnp.concatenate([step, middle], axis=1)
        outer = mm(weighted, inverse).astype(BF16)
        stacks.append(jnp.concatenate([rim, outer], axis=0))
        left = jnp.zeros_like(exact)
        for k in range(each):
            left += exact
            rounded = left.astype(BF16)
            left -= rounded.astype(F32)
            o_ref[e * each + k, chunk:] = rounded
    copies[3].wait()
    for e in range(count):
        columns = mm(stacks[e], b_ref[e]).T.astype(BF16)
        for k in range(each):
            o_ref[e * each + k, :chunk] = columns[k * chunk : (k + 1) * chunk]


SLOTS = 4


def sweep_all(core_ref, mine_ref, other_ref, o_ref, wf_ref, wa_ref, wk_ref):
    strips, chunk, _ = o_ref.shape
    edge = LANES // SLOTS
    groups = strips // SLOTS
    wide = 2 * LANES
    core = core_ref[0]
    skip = 2 * chunk
    evens, odds = range(0, groups, 2), range(1, groups, 2)

    def strip(s, rows):
        return jnp.where(core == s % 2, mine_ref[s // 2, rows], other_ref[s // 2, rows])

    at = lax.broadcasted_iota(jnp.int32, (1, 2 * wide), 1)
    source = ((at >> 7) << 5) | (at & 31)
    spread = lax.broadcasted_iota(jnp.int32, (LANES, 2 * wide), 0) == source
    spread = spread.astype(F32).astype(BF16)
    at = lax.broadcasted_iota(jnp.int32, (wide, 1), 0)
    source = ((at >> 7) << 5) | (at & 31)
    spread_t = lax.broadcasted_iota(jnp.int32, (wide, LANES), 1) == source
    spread_t = spread_t.astype(F32).astype(BF16)
    row_slot = (lax.broadcasted_iota(jnp.int32, (wide, 1), 0) >> 5) & 3
    lane_slot = (lax.broadcasted_iota(jnp.int32, (1, 2 * wide), 1) >> 5) & 3
    same = row_slot == lane_slot
    for g in range(groups):
        stack = jnp.concatenate(
            [
                strip(g + groups * j, slice(skip + a * edge, skip + (a + 1) * edge))
                for a in range(2)
                for j in range(SLOTS)
            ],
            axis=0,
        )
        both = jnp.where(same, mm(stack, spread), 0.0).astype(BF16)
        wf_ref[g] = both[:, :wide]
        wk_ref[g] = both[:, wide:]
        wa_ref[g] = jnp.where(same[:, :wide], mm_nt(spread_t, stack), 0.0).astype(BF16)

    at = lax.broadcasted_iota(jnp.int32, (1, 2 * wide), 1)
    source = (((at >> 5) & 3) << 7) | ((at >> 7) << 5) | (at & 31)
    order = lax.broadcasted_iota(jnp.int32, (2 * wide, 2 * wide), 0) == source
    order = order.astype(F32).astype(BF16)
    mine = pl.ds(pl.multiple_of(core * chunk, chunk), chunk)
    start = jnp.concatenate(
        [
            jnp.concatenate([strip(g + groups * j, mine) for j in range(SLOTS)], axis=1)
            for g in range(groups)
        ],
        axis=0,
    )
    start = mm(start, order)

    def up(parts, at):
        if at == 1:
            return [pltpu.roll(parts[-1], edge, 1)] + parts[:-1]
        return list(parts)

    def down(parts, at):
        if at == 1:
            return list(parts)
        return parts[1:] + [pltpu.roll(parts[0], LANES - edge, 1)]

    def arrive(parts, at, first_up):
        first, second = [v[:, :LANES] for v in parts], [v[:, LANES:] for v in parts]
        if first_up:
            first, second = up(first, at), down(second, at)
        else:
            first, second = down(first, at), up(second, at)
        return [jnp.concatenate([p, q], axis=1).astype(BF16) for p, q in zip(first, second)]

    def iterate(base, weights, first_up):
        even, odd = [base[g] for g in evens], [base[g] for g in odds]
        ahead, behind = odd, even
        z = arrive(ahead, 1, first_up)
        ahead = [even[i] + mm(z[i], weights[g]) for i, g in enumerate(evens)]
        for t in range(1, SWEEPS - 2):
            at = (t + 1) % 2
            z = arrive(ahead, at, first_up)
            y = arrive(behind, at, first_up)
            add = odd if at == 0 else even
            both = []
            for i, g in enumerate(odds if at == 0 else evens):
                both.append(mm(jnp.concatenate([z[i], y[i]], axis=0), weights[g]))
            ahead = [add[i] + v[:chunk] for i, v in enumerate(both)]
            behind = [add[i] + v[chunk:] for i, v in enumerate(both)]
        at = (SWEEPS - 1) % 2
        y = arrive(behind, at, first_up)
        add = odd if at == 0 else even
        behind = [
            add[i] + mm(y[i], weights[g]) for i, g in enumerate(odds if at == 0 else evens)
        ]
        gets_ahead, gets_behind = arrive(ahead, at, first_up), arrive(behind, 1 - at, first_up)
        got = [None] * groups
        for i, g in enumerate(odds if at == 0 else evens):
            got[g] = gets_ahead[i]
        for i, g in enumerate(evens if at == 0 else odds):
            got[g] = gets_behind[i]
        return got

    base = [start[g * chunk : (g + 1) * chunk, :wide] for g in range(groups)]
    z = iterate(base, wf_ref, True)
    base = [
        start[g * chunk : (g + 1) * chunk, wide:] + mm(z[g], wk_ref[g]) for g in range(groups)
    ]
    y = iterate(base, wa_ref, False)
    out = jnp.concatenate(
        [jnp.concatenate([z[g], y[g]], axis=1) for g in range(groups)], axis=0
    )
    out = mm(out, order).astype(BF16)
    for g in range(groups):
        for j in range(SLOTS):
            o_ref[g + groups * j] = out[g * chunk : (g + 1) * chunk, j * LANES : (j + 1) * LANES]


def finish(w_ref, low_ref, high_ref, p_ref, b_ref, l_ref, r_ref, zy_ref, o_ref):
    count, block, modes = b_ref.shape
    edge = l_ref.shape[0]
    couple = jnp.concatenate([l_ref[...], r_ref[...]], axis=0).astype(F32).T.astype(BF16)
    couple = jnp.concatenate([couple, jnp.zeros_like(couple)], axis=1)
    inside = collector_row(low_ref, high_ref, (block, 1), 0)
    pick = (
        lax.broadcasted_iota(jnp.int32, (2 * edge, LANES), 0) + 2 * edge
        == lax.broadcasted_iota(jnp.int32, (2 * edge, LANES), 1)
    ).astype(F32).astype(BF16)
    total = jnp.zeros((block, block), F32)
    for e in range(count):
        inverse = p_ref[e]
        got = mm_nt(jnp.concatenate([couple, pick], axis=0), zy_ref[e])
        rhs = (b_ref[e].astype(F32) + got[:block]).astype(BF16)
        psi = mm(inverse, rhs).astype(BF16)
        source = jnp.where(inside, psi.astype(F32) * (2.0 * w_ref[e]), 0.0)
        update = jnp.concatenate(
            [
                source[:edge] + got[block + edge :],
                source[edge : block - edge],
                source[block - edge :] + got[block : block + edge],
            ],
            axis=0,
        ).astype(BF16)
        lam = lax.dot_general(
            inverse, update, (((0,), (0,)), ((), ())), preferred_element_type=F32
        ).astype(BF16)
        total += mm_nt(lam, psi)
    total = (total * (-1.0 / modes)).astype(BF16)
    pieces, owned, _ = o_ref.shape
    for k in range(pieces):
        o_ref[k] = total[k * owned : (k + 1) * owned]


SMEM = pl.BlockSpec(memory_space=pltpu.SMEM)
VMEM = pl.BlockSpec(memory_space=pltpu.VMEM)
ANY = pl.BlockSpec(memory_space=pltpu.HBM)
PARAMS = dict(compiler_params=pltpu.CompilerParams(vmem_limit_bytes=24 * 1024 * 1024))


def body(
    inverse_blocks,
    source,
    left_coupling,
    right_coupling,
    energy_weights,
    collector_low,
    collector_high,
):
    count, block, modes = source.shape
    edge = left_coupling.shape[0]
    chips = lax.axis_size("chip")
    cores = lax.axis_size("core")
    strips = chips * cores
    energies = lax.axis_size("energy")
    chunk = count * modes // strips
    owned = block // energies
    scalars = (energy_weights, collector_low, collector_high)
    shape = jax.ShapeDtypeStruct

    pieces = pl.pallas_call(
        prepare,
        out_shape=shape((chips, cores * chunk + 2 * edge, 4 * edge), BF16),
        in_specs=[SMEM] * 3 + [ANY] * 4,
        out_specs=VMEM,
        scratch_shapes=[
            pltpu.VMEM((count, block, block), BF16),
            pltpu.VMEM((count, block, modes), BF16),
            pltpu.VMEM((2 * edge, block), BF16),
            pltpu.SemaphoreType.DMA((4,)),
        ],
        name="prepare",
    )(*scalars, inverse_blocks, source, left_coupling, right_coupling)
    mine = lax.all_to_all(pieces, "chip", 0, 0, tiled=True)
    other = lax.ppermute(mine, "core", [(i, cores - 1 - i) for i in range(cores)])
    core = lax.axis_index("core").astype(jnp.int32).reshape(1)
    weights = pltpu.VMEM((strips // SLOTS, 2 * LANES, 2 * LANES), BF16)
    out = pl.pallas_call(
        sweep_all,
        out_shape=shape((strips, chunk, 4 * edge), BF16),
        in_specs=[SMEM] + [VMEM] * 2,
        out_specs=VMEM,
        scratch_shapes=[weights] * 3,
        name="sweeps",
        **PARAMS,
    )(core, mine, other)
    out = lax.all_to_all(out, ("chip", "core"), 0, 0, tiled=True)
    out = pl.pallas_call(
        finish,
        out_shape=shape((energies, owned, block), BF16),
        in_specs=[SMEM] * 3 + [VMEM] * 5,
        out_specs=VMEM,
        name="finish",
        **PARAMS,
    )(
        *scalars,
        inverse_blocks,
        source,
        left_coupling,
        right_coupling,
        out.reshape(count, modes, 4 * edge),
    )
    out = lax.all_to_all(out, "energy", 0, 0, tiled=True)
    return jnp.sum(out.astype(F32), axis=0)[None]


def solution(mesh):
    energies, strips = mesh.devices.shape
    cores = 2
    split = jax.sharding.Mesh(
        mesh.devices.reshape(energies, strips // cores, cores), ("energy", "chip", "core")
    )
    width = ("chip", "core")
    placed = (
        P("energy", width, None),
        P("energy", width, None),
        P(width, None),
        P(width, None),
        P("energy"),
        P(width),
        P(width),
    )
    return jax.shard_map(
        body, mesh=split, in_specs=placed, out_specs=P(width, "energy", None), check_vma=False
    )
```

time: 459 us -> 80.7 us (0.18)
  waiting for transfers between devices: 340 us -> 1.87 us
  starting transfers between devices: 78.2 us -> 1.91 us
  blocking collectives: 0 us -> 63.4 us
  matrix products: 16.6 us -> 0 us
  between operations: 14.8 us -> 1.36 us
  Pallas kernels: 0 us -> 10.6 us
    psum x1 -> x0, waiting for transfers between devices: 170 us -> none  [body(): full = lax.psum(product * (-1.0 / modes), 'energy')]
    ppermute x36 -> x1, waiting for transfers between devices: 170 us -> 1.87 us  [body(): lax.ppermute(mine, 'core', [(i, cores - 1 - i) for i in range(cores)])]
    ppermute x36 -> x1, starting transfers between devices: 78.2 us -> 1.91 us  [body(): lax.ppermute(mine, 'core', [(i, cores - 1 - i) for i in range(cores)])]
    all_to_all x0 -> x3, blocking collectives: none -> 63.4 us  [the longest x1 28.3 us: body(): mine = lax.all_to_all(pieces, 'chip', 0, 0, tiled=True)]
    dot_general x48 -> x0, matrix products: 16.6 us -> none  [the longest x9 4.72 us: forward_sweep(): jnp.einsum('kij,kjm->kim', inverse_blocks, rhs, preferred_element_type=jn...]
    pallas_call x0 -> x3, Pallas kernels: none -> 10.6 us  [the longest x1 5.28 us: body(): pl.pallas_call(sweep_all, out_shape=shape((strips, chunk, 4 * edge), BF16...]
  transfers between devices with their start and end apart: 37 -> 1, of which waited for: 37 -> 1; matrix products, arithmetic and copies ran while one was open for 1% -> 0% of each run, Pallas kernels for 0% -> 0%
where the time goes in v1:
time: 80.7 us; the launch traced here: 80.4 us
  blocking collectives  63.4 us (79%)
  Pallas kernels  10.6 us (13%)
  starting transfers between devices  1.91 us (2%)
  waiting for transfers between devices  1.87 us (2%)
  between operations  1.36 us (2%)
    all_to_all x1, blocking collectives, body(): mine = lax.all_to_all(pieces, 'chip', 0, 0, tiled=True)  28.3 us
    all_to_all x1, blocking collectives, body(): out = lax.all_to_all(out, 'energy', 0, 0, tiled=True)  19.3 us
    all_to_all x1, blocking collectives, body(): out = lax.all_to_all(out, ('chip', 'core'), 0, 0, tiled=True)  15.7 us
    pallas_call x1, Pallas kernels, body(): pl.pallas_call(sweep_all, out_shape=shape((strips, chunk, 4 * edge), BF16...  5.28 us
    pallas_call x1, Pallas kernels, body(): pl.pallas_call(prepare, out_shape=shape((chips, cores * chunk + 2 * edge,...  3.29 us
    pallas_call x1, Pallas kernels, body(): pl.pallas_call(finish, out_shape=shape((energies, owned, block), BF16), i...  2.01 us
    ppermute x1, starting transfers between devices, body(): lax.ppermute(mine, 'core', [(i, cores - 1 - i) for i in range(cores)])  1.91 us
    ppermute x1, waiting for transfers between devices, body(): lax.ppermute(mine, 'core', [(i, cores - 1 - i) for i in range(cores)])  1.87 us
  transfers between devices with their start and end apart: 1, of which 1 were waited for; matrix products, arithmetic and copies ran while one was open for 0% of the time, Pallas kernels for 0%

profile of v1, /device:TPU:8, one launch (start us, length us, event | category | flops | bytes accessed | tf_op | source)
XLA Modules:
  0.0 80.4 jit_solution(1134970349159587581)
XLA Ops:
  1.3 3.3 %prepare.1 = bf16[16,128,128]{2,1,0:T(8,128)(2,1)} custom-call(f32[2]{0:T(128)} %w_ref.3, s32[1]{0:T(128)S(6)} %copy.8.low_ref, s32[1]{0:T(128)S(6)} %copy.9.high_ref, bf16[2,256,256]{2,1,0:T(8,128)(2,1)} %p_ref.1, bf16[2,256,512]{2,1,0:T(8,128)(2,1)} %b_ref.1, bf16[32,256]{1,0:T(8,128)(2,1)} %l_ref.1, bf16[32,256]{1,0:T(8,128)(2,1)} %r_ref.1), custom_call_target="tpu_custom_call" | custom-call | tf_op jit(solution)/shard_map/prepare/pallas_call | solution.py:247
  4.6 28.3 %all_to_all.15.mine_ref = bf16[16,128,128]{2,1,0:T(8,128)(2,1)S(1)} all-to-all(bf16[16,128,128]{2,1,0:T(8,128)(2,1)} %prepare.1), channel_id=1, replica_groups=mesh['energy'=16,'chip'=16,'core'=2] {'chip'}, dimensions={0} | all-to-all | bytes 1048576 | tf_op jit(solution)/shard_map/all_to_all | solution.py:260
  32.9 1.9 %collective-permute-start = (bf16[16,128,128]{2,1,0:T(8,128)(2,1)S(1)}, bf16[16,128,128]{2,1,0:T(8,128)(2,1)S(1)}, u32[]{:S(2)}, u32[]{:S(2)}) collective-permute-start(bf16[16,128,128]{2,1,0:T(8,128)(2,1)S(1)} %all_to_all.15.mine_ref), channel_id=1, source_target_pairs={{0,1},{1,0},{2,3},{3,2},{4,5},{5,4},{6,7},{7,6},{8,9},{9,8},{10,11... | collective-permute-start | bytes 1572872 | tf_op jit(solution)/shard_map/ppermute | solution.py:261
  34.8 1.9 %collective-permute-done.other_ref = bf16[16,128,128]{2,1,0:T(8,128)(2,1)S(1)} collective-permute-done((bf16[16,128,128]{2,1,0:T(8,128)(2,1)S(1)}, bf16[16,128,128]{2,1,0:T(8,128)(2,1)S(1)}, u32[]{:S(2)}, u32[]{:S(2)}) %collective-permute-start) | collective-permute-done | bytes 524320 | tf_op jit(solution)/shard_map/ppermute | solution.py:261
  36.7 0.0 copy-start.1
  36.7 0.0 copy-start.2
  36.7 0.0 copy-start.3
  36.7 5.3 %sweeps.1 = bf16[32,32,128]{2,1,0:T(8,128)(2,1)S(1)} custom-call(s32[1]{0:T(128)} %bitcast.core_ref, bf16[16,128,128]{2,1,0:T(8,128)(2,1)S(1)} %all_to_all.15.mine_ref, bf16[16,128,128]{2,1,0:T(8,128)(2,1)S(1)} %collective-permute-done.other_ref), custom_call_target="tpu_custom_call" | custom-call | tf_op jit(solution)/shard_map/sweeps/pallas_call | solution.py:264
  42.0 0.0 copy-start
  42.0 15.7 %all_to_all.16 = bf16[32,32,128]{2,1,0:T(8,128)(2,1)S(1)} all-to-all(bf16[32,32,128]{2,1,0:T(8,128)(2,1)S(1)} %sweeps.1), channel_id=1, replica_groups=mesh['energy'=16,'chip'=16,'core'=2] {'chip','core'}, dimensions={0} | all-to-all | bytes 524288 | tf_op jit(solution)/shard_map/all_to_all | solution.py:273
  57.8 0.0 copy-start.4
  57.8 0.0 copy-done.1
  57.8 0.0 copy-done.2
  57.8 0.0 copy-done.3
  57.8 0.0 copy-done
  57.8 0.6 copy-done.4
  58.4 2.0 %finish.1 = bf16[16,16,256]{2,1,0:T(8,128)(2,1)S(1)} custom-call(f32[2]{0:T(128)S(1)} %copy-done.4, s32[1]{0:T(128)S(6)} %copy.8.low_ref, s32[1]{0:T(128)S(6)} %copy.9.high_ref, bf16[2,256,256]{2,1,0:T(8,128)(2,1)S(1)} %copy-done.1, bf16[2,256,512]{2,1,0:T(8,128)(2,1)S(1)} %copy-done, bf16[32,256]{1,0:T(8,128)(2,1)S(1)} %copy-done.2, ...), custom_call_target="tpu_custom_call" | custom-call | tf_op jit(solution)/shard_map/finish/pallas_call | solution.py:274
  60.4 19.3 %all_to_all.17 = bf16[16,16,256]{2,1,0:T(8,128)(2,1)S(1)} all-to-all(bf16[16,16,256]{2,1,0:T(8,128)(2,1)S(1)} %finish.1), channel_id=1, replica_groups=mesh['energy'=16,'chip'=16,'core'=2] {'energy'}, dimensions={0} | all-to-all | bytes 262144 | tf_op jit(solution)/shard_map/all_to_all | solution.py:289
  79.7 0.6 convert_reduce_fusion
Async XLA Ops:
  32.9 3.8 %collective-permute-start = (bf16[16,128,128]{2,1,0:T(8,128)(2,1)S(1)}, bf16[16,128,128]{2,1,0:T(8,128)(2,1)S(1)}, u32[]{:S(2)}, u32[]{:S(2)}) collective-permute-start(bf16[16,128,128]{2,1,0:T(8,128)(2,1)S(1)} %all_to_all.15.mine_ref), channel_id=1, source_target_pairs={{0,1},{1,0},{2,3},{3,2},{4,5},{5,4},{6,7},{7,6},{8,9},{9,8},{10,11... | collective-permute-start | bytes 1572872 | tf_op jit(solution)/shard_map/ppermute | solution.py:261
  36.7 21.1 %copy-start.1 = (bf16[2,256,256]{2,1,0:T(8,128)(2,1)S(1)}, bf16[2,256,256]{2,1,0:T(8,128)(2,1)}, u32[]{:S(2)}) copy-start(bf16[2,256,256]{2,1,0:T(8,128)(2,1)} %p_ref.1) | copy-start | bytes 786436
  36.7 21.1 %copy-start.2 = (bf16[32,256]{1,0:T(8,128)(2,1)S(1)}, bf16[32,256]{1,0:T(8,128)(2,1)}, u32[]{:S(2)}) copy-start(bf16[32,256]{1,0:T(8,128)(2,1)} %l_ref.1) | copy-start | bytes 49156
  36.7 21.1 %copy-start.3 = (bf16[32,256]{1,0:T(8,128)(2,1)S(1)}, bf16[32,256]{1,0:T(8,128)(2,1)}, u32[]{:S(2)}) copy-start(bf16[32,256]{1,0:T(8,128)(2,1)} %r_ref.1) | copy-start | bytes 49156
  42.0 15.8 %copy-start = (bf16[2,256,512]{2,1,0:T(8,128)(2,1)S(1)}, bf16[2,256,512]{2,1,0:T(8,128)(2,1)}, u32[]{:S(2)}) copy-start(bf16[2,256,512]{2,1,0:T(8,128)(2,1)} %b_ref.1) | copy-start | bytes 1572868
  57.8 0.7 copy-start.4

commit v2 on v1

v2 whole, which is shorter than its diff:
```python
import jax
import jax.numpy as jnp
from jax import lax
from jax.experimental import pallas as pl
from jax.experimental.pallas import tpu as pltpu
from jax.sharding import PartitionSpec as P

SWEEPS = 10
LANES = 128
F32 = jnp.float32
BF16 = jnp.bfloat16


def mm(a, b):
    return jnp.dot(a, b, preferred_element_type=F32)


def mm_nt(a, b):
    return lax.dot_general(a, b, (((1,), (1,)), ((), ())), preferred_element_type=F32)


def prepare(
    w_hbm,
    low_hbm,
    high_hbm,
    p_hbm,
    b_hbm,
    l_hbm,
    r_hbm,
    o_hbm,
    scale_hbm,
    w_ref,
    low_ref,
    high_ref,
    p_ref,
    b_ref,
    c_ref,
    o_ref,
    scale_ref,
    sems,
):
    count, block, modes = b_ref.shape
    edge = l_hbm.shape[0]
    fetch = [
        (w_hbm, w_ref),
        (low_hbm, low_ref),
        (high_hbm, high_ref),
        (l_hbm, c_ref.at[pl.ds(0, edge)]),
        (r_hbm, c_ref.at[pl.ds(edge, edge)]),
        (p_hbm, p_ref),
        (b_hbm, b_ref),
    ]
    fetch = [pltpu.make_async_copy(*ends, sems.at[i]) for i, ends in enumerate(fetch)]
    for copy in fetch:
        copy.start()
    for copy in fetch[:3]:
        copy.wait()
    low, high = low_ref[0], high_ref[0]
    at = lax.broadcasted_iota(jnp.int32, (block, LANES), 0)
    inside = (at >= low) & (at < high)
    for e in range(count):
        scale_ref[e] = jnp.where(inside, 2.0 * w_ref[e], 0.0)
    keep = [pltpu.make_async_copy(scale_ref, scale_hbm, sems.at[len(fetch)])]
    keep[0].start()
    at = lax.broadcasted_iota(jnp.int32, (1, block), 1)
    inside = (at >= low) & (at < high)
    for copy in fetch[3:6]:
        copy.wait()
    couple = c_ref[...]
    chunk = o_ref.shape[1] - 2 * edge
    each = modes // chunk
    energies = range(count)
    rim = [jnp.concatenate([p_ref[e, block - edge :], p_ref[e, :edge]], axis=0) for e in energies]
    u = [mm_nt(couple, p_ref[e]) for e in energies]
    step = [mm_nt(couple, rim[e]) for e in energies]
    weighted = [jnp.where(inside, u[e] * (2.0 * w_ref[e]), 0.0).astype(BF16) for e in energies]
    outer = [mm(weighted[e], p_ref[e]).astype(BF16) for e in energies]
    middle = [mm_nt(weighted[e], u[e].astype(BF16)) for e in energies]
    fetch[6].wait()
    for e in energies:
        rows = mm(jnp.concatenate([rim[e], outer[e]], axis=0), b_ref[e])
        columns = rows.T.astype(BF16)
        exact = jnp.concatenate([step[e], middle[e]], axis=1)
        left = jnp.zeros_like(exact)
        for k in range(each):
            left += exact
            rounded = left.astype(BF16)
            left -= rounded.astype(F32)
            o_ref[e * each + k, chunk:] = rounded
            o_ref[e * each + k, :chunk] = columns[k * chunk : (k + 1) * chunk]
        part = pl.ds(e * each, each)
        keep.append(
            pltpu.make_async_copy(o_ref.at[part], o_hbm.at[part], sems.at[len(fetch) + 1 + e])
        )
        keep[-1].start()
    for copy in keep:
        copy.wait()


SLOTS = 4


def sweep_all(core_ref, mine_ref, other_ref, o_ref, wf_ref, wa_ref, wk_ref):
    strips, chunk, _ = o_ref.shape
    edge = LANES // SLOTS
    groups = strips // SLOTS
    wide = 2 * LANES
    core = core_ref[0]
    skip = 2 * chunk
    evens, odds = range(0, groups, 2), range(1, groups, 2)

    def strip(s, rows):
        return jnp.where(core == s % 2, mine_ref[s // 2, rows], other_ref[s // 2, rows])

    at = lax.broadcasted_iota(jnp.int32, (1, 2 * wide), 1)
    source = ((at >> 7) << 5) | (at & 31)
    spread = lax.broadcasted_iota(jnp.int32, (LANES, 2 * wide), 0) == source
    spread = spread.astype(F32).astype(BF16)
    at = lax.broadcasted_iota(jnp.int32, (wide, 1), 0)
    source = ((at >> 7) << 5) | (at & 31)
    spread_t = lax.broadcasted_iota(jnp.int32, (wide, LANES), 1) == source
    spread_t = spread_t.astype(F32).astype(BF16)
    row_slot = (lax.broadcasted_iota(jnp.int32, (wide, 1), 0) >> 5) & 3
    lane_slot = (lax.broadcasted_iota(jnp.int32, (1, 2 * wide), 1) >> 5) & 3
    def stacked(g, turns):
        return jnp.concatenate(
            [
                strip(
                    g + groups * ((j + turns[a]) % SLOTS),
                    slice(skip + a * edge, skip + (a + 1) * edge),
                )
                for a in range(2)
                for j in range(SLOTS)
            ],
            axis=0,
        )

    def matching(turns, lanes):
        half = lax.broadcasted_iota(jnp.int32, (wide, 1), 0) >> 7
        slot = row_slot + jnp.where(half == 0, turns[0], turns[1])
        return (slot & 3) == lane_slot[:, :lanes]

    last = groups - 1
    for g in range(groups):
        turns = {0: (1, 0), last: (0, -1)}.get(g, (0, 0))
        back = {0: (0, 1), last: (-1, 0)}.get(g, (0, 0))
        both = mm(stacked(g, turns), spread)
        both = jnp.where(matching(turns, 2 * wide), both, 0.0).astype(BF16)
        wf_ref[g] = both[:, :wide]
        wk_ref[g] = both[:, wide:]
        both = mm_nt(spread_t, stacked(g, (0, 0)))
        wa_ref[g] = jnp.where(matching(back, wide), both, 0.0).astype(BF16)

    at = lax.broadcasted_iota(jnp.int32, (1, 2 * wide), 1)
    source = (((at >> 5) & 3) << 7) | ((at >> 7) << 5) | (at & 31)
    order = lax.broadcasted_iota(jnp.int32, (2 * wide, 2 * wide), 0) == source
    order = order.astype(F32).astype(BF16)
    mine = pl.ds(pl.multiple_of(core * chunk, chunk), chunk)
    start = jnp.concatenate(
        [
            jnp.concatenate([strip(g + groups * j, mine) for j in range(SLOTS)], axis=1)
            for g in range(groups)
        ],
        axis=0,
    )
    start = mm(start, order)

    def up(parts, at):
        return [parts[-1]] + parts[:-1] if at == 1 else list(parts)

    def down(parts, at):
        return list(parts) if at == 1 else parts[1:] + [parts[0]]

    def arrive(parts, at, first_up):
        first, second = [v[:, :LANES] for v in parts], [v[:, LANES:] for v in parts]
        if first_up:
            first, second = up(first, at), down(second, at)
        else:
            first, second = down(first, at), up(second, at)
        return [jnp.concatenate([p, q], axis=1).astype(BF16) for p, q in zip(first, second)]

    def turned(parts, first_up):
        def turn(part, half, by):
            halves = [part[:, :LANES], part[:, LANES:]]
            halves[half] = pltpu.roll(halves[half].astype(F32), by, 1).astype(BF16)
            return jnp.concatenate(halves, axis=1)

        parts = list(parts)
        parts[0] = turn(parts[0], 0 if first_up else 1, edge)
        parts[last] = turn(parts[last], 1 if first_up else 0, LANES - edge)
        return parts

    def iterate(base, weights, first_up):
        even, odd = [base[g] for g in evens], [base[g] for g in odds]
        ahead, behind = odd, even
        z = arrive(ahead, 1, first_up)
        ahead = [even[i] + mm(z[i], weights[g]) for i, g in enumerate(evens)]
        for t in range(1, SWEEPS - 2):
            at = (t + 1) % 2
            z = arrive(ahead, at, first_up)
            y = arrive(behind, at, first_up)
            add = odd if at == 0 else even
            both = []
            for i, g in enumerate(odds if at == 0 else evens):
                both.append(mm(jnp.concatenate([z[i], y[i]], axis=0), weights[g]))
            ahead = [add[i] + v[:chunk] for i, v in enumerate(both)]
            behind = [add[i] + v[chunk:] for i, v in enumerate(both)]
        at = (SWEEPS - 1) % 2
        y = arrive(behind, at, first_up)
        add = odd if at == 0 else even
        behind = [
            add[i] + mm(y[i], weights[g]) for i, g in enumerate(odds if at == 0 else evens)
        ]
        gets_ahead, gets_behind = arrive(ahead, at, first_up), arrive(behind, 1 - at, first_up)
        got = [None] * groups
        for i, g in enumerate(odds if at == 0 else evens):
            got[g] = gets_ahead[i]
        for i, g in enumerate(evens if at == 0 else odds):
            got[g] = gets_behind[i]
        return got

    base = [start[g * chunk : (g + 1) * chunk, :wide] for g in range(groups)]
    z = iterate(base, wf_ref, True)
    base = [
        start[g * chunk : (g + 1) * chunk, wide:] + mm(z[g], wk_ref[g]) for g in range(groups)
    ]
    y = iterate(base, wa_ref, False)
    z, y = turned(z, True), turned(y, False)
    out = jnp.concatenate(
        [jnp.concatenate([z[g], y[g]], axis=1) for g in range(groups)], axis=0
    )
    out = mm(out, order).astype(BF16)
    for g in range(groups):
        for j in range(SLOTS):
            o_ref[g + groups * j] = out[g * chunk : (g + 1) * chunk, j * LANES : (j + 1) * LANES]


def finish(scale_ref, p_ref, b_ref, l_ref, r_ref, zy_ref, o_ref):
    count, block, modes = b_ref.shape
    edge = l_ref.shape[0]
    couple = jnp.concatenate([l_ref[...], r_ref[...]], axis=0).astype(F32).T.astype(BF16)
    couple = jnp.concatenate([couple, jnp.zeros_like(couple)], axis=1)
    pick = (
        lax.broadcasted_iota(jnp.int32, (2 * edge, LANES), 0) + 2 * edge
        == lax.broadcasted_iota(jnp.int32, (2 * edge, LANES), 1)
    ).astype(F32).astype(BF16)
    front = jnp.concatenate([couple, pick], axis=0)
    energies = range(count)
    got = [mm_nt(front, zy_ref[e]) for e in energies]
    rhs = [(b_ref[e].astype(F32) + got[e][:block]).astype(BF16) for e in energies]
    psi = [mm(p_ref[e], rhs[e]).astype(BF16) for e in energies]
    scale = [jnp.concatenate([scale_ref[e]] * (modes // LANES), axis=1) for e in energies]
    source = [psi[e].astype(F32) * scale[e] for e in energies]
    update = [
        jnp.concatenate(
            [
                source[e][:edge] + got[e][block + edge :],
                source[e][edge : block - edge],
                source[e][block - edge :] + got[e][block : block + edge],
            ],
            axis=0,
        ).astype(BF16)
        for e in energies
    ]
    total = jnp.zeros((block, block), F32)
    for e in energies:
        part = mm_nt(update[e], psi[e])
        high = part.astype(BF16)
        low = (part - high.astype(F32)).astype(BF16)
        inverse_t = p_ref[e].T
        total += mm(inverse_t, high) + mm(inverse_t, low)
    total = (total * (-1.0 / modes)).astype(BF16)
    pieces, owned, _ = o_ref.shape
    for k in range(pieces):
        o_ref[k] = total[k * owned : (k + 1) * owned]


SMEM = pl.BlockSpec(memory_space=pltpu.SMEM)
VMEM = pl.BlockSpec(memory_space=pltpu.VMEM)
ANY = pl.BlockSpec(memory_space=pltpu.HBM)
PARAMS = dict(compiler_params=pltpu.CompilerParams(vmem_limit_bytes=24 * 1024 * 1024))


shape = jax.ShapeDtypeStruct


def call_prepare(scalars, inverse, source, left, right, chips, cores, chunk):
    count, block, modes = source.shape
    edge = left.shape[0]
    pieces = (chips, cores * chunk + 2 * edge, 4 * edge)
    return pl.pallas_call(
        prepare,
        out_shape=(shape(pieces, BF16), shape((count, block, LANES), F32)),
        in_specs=[ANY] * 7,
        out_specs=(ANY, ANY),
        scratch_shapes=[
            pltpu.SMEM((count,), F32),
            pltpu.SMEM((1,), jnp.int32),
            pltpu.SMEM((1,), jnp.int32),
            pltpu.VMEM((count, block, block), BF16),
            pltpu.VMEM((count, block, modes), BF16),
            pltpu.VMEM((2 * edge, block), BF16),
            pltpu.VMEM(pieces, BF16),
            pltpu.VMEM((count, block, LANES), F32),
            pltpu.SemaphoreType.DMA((8 + count,)),
        ],
        name="prepare",
    )(*scalars, inverse, source, left, right)


def call_sweeps(core, mine, other):
    chips, rows, lanes = mine.shape
    strips = 2 * chips
    chunk = (rows - 2 * lanes // SLOTS) // 2
    weights = pltpu.VMEM((strips // SLOTS, 2 * LANES, 2 * LANES), BF16)
    return pl.pallas_call(
        sweep_all,
        out_shape=shape((strips, chunk, lanes), BF16),
        in_specs=[SMEM] + [VMEM] * 2,
        out_specs=VMEM,
        scratch_shapes=[weights] * 3,
        name="sweeps",
        **PARAMS,
    )(core, mine, other)


def call_finish(scale, inverse, source, left, right, columns, energies, owned):
    block = inverse.shape[1]
    return pl.pallas_call(
        finish,
        out_shape=shape((energies, owned, block), BF16),
        in_specs=[VMEM] * 6,
        out_specs=VMEM,
        name="finish",
        **PARAMS,
    )(scale, inverse, source, left, right, columns)


def body(
    inverse_blocks,
    source,
    left_coupling,
    right_coupling,
    energy_weights,
    collector_low,
    collector_high,
):
    count, block, modes = source.shape
    edge = left_coupling.shape[0]
    chips = lax.axis_size("chip")
    cores = lax.axis_size("core")
    strips = chips * cores
    energies = lax.axis_size("energy")
    chunk = count * modes // strips
    owned = block // energies
    scalars = (energy_weights, collector_low, collector_high)

    pieces, scale = call_prepare(
        scalars, inverse_blocks, source, left_coupling, right_coupling, chips, cores, chunk
    )
    mine = lax.all_to_all(pieces, "chip", 0, 0, tiled=True)
    other = lax.ppermute(mine, "core", [(i, cores - 1 - i) for i in range(cores)])
    core = lax.axis_index("core").astype(jnp.int32).reshape(1)
    out = call_sweeps(core, mine, other)
    out = lax.all_to_all(out, ("chip", "core"), 0, 0, tiled=True)
    out = call_finish(
        scale,
        inverse_blocks,
        source,
        left_coupling,
        right_coupling,
        out.reshape(count, modes, 4 * edge),
        energies,
        owned,
    )
    out = lax.all_to_all(out, "energy", 0, 0, tiled=True)
    return jnp.sum(out.astype(F32), axis=0)[None]


def solution(mesh):
    energies, strips = mesh.devices.shape
    cores = 2
    split = jax.sharding.Mesh(
        mesh.devices.reshape(energies, strips // cores, cores), ("energy", "chip", "core")
    )
    width = ("chip", "core")
    placed = (
        P("energy", width, None),
        P("energy", width, None),
        P(width, None),
        P(width, None),
        P("energy"),
        P(width),
        P(width),
    )
    return jax.shard_map(
        body, mesh=split, in_specs=placed, out_specs=P(width, "energy", None), check_vma=False
    )
```

time: 80.7 us -> 77.8 us (0.964)
  Pallas kernels: 10.6 us -> 8.32 us
    pallas_call x3, Pallas kernels: 10.6 us -> 8.32 us  [the longest x1 4.68 us: call_sweeps(): pl.pallas_call(sweep_all, out_shape=shape((strips, chunk, lanes), BF16),...]
where the time goes in v2:
time: 77.8 us; the launch traced here: 77.5 us
  blocking collectives  63.4 us (81%)
  Pallas kernels  8.32 us (11%)
  starting transfers between devices  1.91 us (2%)
  waiting for transfers between devices  1.87 us (2%)
  between operations  1.37 us (2%)
    all_to_all x1, blocking collectives, body(): mine = lax.all_to_all(pieces, 'chip', 0, 0, tiled=True)  28.3 us
    all_to_all x1, blocking collectives, body(): out = lax.all_to_all(out, 'energy', 0, 0, tiled=True)  19.3 us
    all_to_all x1, blocking collectives, body(): out = lax.all_to_all(out, ('chip', 'core'), 0, 0, tiled=True)  15.7 us
    pallas_call x1, Pallas kernels, call_sweeps(): pl.pallas_call(sweep_all, out_shape=shape((strips, chunk, lanes), BF16),...  4.68 us
    pallas_call x1, Pallas kernels, call_prepare(): pl.pallas_call(prepare, out_shape=(shape(pieces, BF16), shape((count, blo...  2.5 us
    ppermute x1, starting transfers between devices, body(): lax.ppermute(mine, 'core', [(i, cores - 1 - i) for i in range(cores)])  1.91 us
    ppermute x1, waiting for transfers between devices, body(): lax.ppermute(mine, 'core', [(i, cores - 1 - i) for i in range(cores)])  1.87 us
  transfers between devices with their start and end apart: 1, of which 1 were waited for; matrix products, arithmetic and copies ran while one was open for 0% of the time, Pallas kernels for 0%

profile of v2, /device:TPU:8, one launch (start us, length us, event | category | flops | bytes accessed | tf_op | source)
XLA Modules:
  0.0 77.5 jit_solution(9181473812955251982)
XLA Ops:
  1.3 2.5 %prepare.1 = (bf16[16,128,128]{2,1,0:T(8,128)(2,1)}, f32[2,256,128]{2,1,0:T(8,128)}) custom-call(f32[2]{0:T(128)} %w_hbm.1, s32[1]{0:T(128)S(6)} %copy.8.low_hbm, s32[1]{0:T(128)S(6)} %copy.9.high_hbm, bf16[2,256,256]{2,1,0:T(8,128)(2,1)} %p_ref.1, bf16[2,256,512]{2,1,0:T(8,128)(2,1)} %b_ref.1, bf16[32,256]{1,0:T(8,128)(2,1)} %l_ref.1, bf16[32,256]{1,0:T(8,128)(2,1)} %r_ref.1), custom_call_target="tpu_custom_call" | custom-call | tf_op jit(solution)/shard_map/prepare/pallas_call | solution.py:291
  3.8 28.3 %all_to_all.15.mine_ref = bf16[16,128,128]{2,1,0:T(8,128)(2,1)S(1)} all-to-all(bf16[16,128,128]{2,1,0:T(8,128)(2,1)} %get-tuple-element.8), channel_id=1, replica_groups=mesh['energy'=16,'chip'=16,'core'=2] {'chip'}, dimensions={0} | all-to-all | bytes 1048576 | tf_op jit(solution)/shard_map/all_to_all | solution.py:361
  32.1 1.9 %collective-permute-start = (bf16[16,128,128]{2,1,0:T(8,128)(2,1)S(1)}, bf16[16,128,128]{2,1,0:T(8,128)(2,1)S(1)}, u32[]{:S(2)}, u32[]{:S(2)}) collective-permute-start(bf16[16,128,128]{2,1,0:T(8,128)(2,1)S(1)} %all_to_all.15.mine_ref), channel_id=1, source_target_pairs={{0,1},{1,0},{2,3},{3,2},{4,5},{5,4},{6,7},{7,6},{8,9},{9,8},{10,11... | collective-permute-start | bytes 1572872 | tf_op jit(solution)/shard_map/ppermute | solution.py:362
  34.1 1.9 %collective-permute-done.other_ref = bf16[16,128,128]{2,1,0:T(8,128)(2,1)S(1)} collective-permute-done((bf16[16,128,128]{2,1,0:T(8,128)(2,1)S(1)}, bf16[16,128,128]{2,1,0:T(8,128)(2,1)S(1)}, u32[]{:S(2)}, u32[]{:S(2)}) %collective-permute-start) | collective-permute-done | bytes 524320 | tf_op jit(solution)/shard_map/ppermute | solution.py:362
  35.9 0.0 copy-start.1
  35.9 0.0 copy-start.2
  35.9 0.0 copy-start.3
  35.9 0.0 copy-start.4
  35.9 4.7 %sweeps.1 = bf16[32,32,128]{2,1,0:T(8,128)(2,1)S(1)} custom-call(s32[1]{0:T(128)} %bitcast.core_ref, bf16[16,128,128]{2,1,0:T(8,128)(2,1)S(1)} %all_to_all.15.mine_ref, bf16[16,128,128]{2,1,0:T(8,128)(2,1)S(1)} %collective-permute-done.other_ref), custom_call_target="tpu_custom_call" | custom-call | tf_op jit(solution)/shard_map/sweeps/pallas_call | solution.py:316
  40.6 0.0 copy-start
  40.6 15.7 %all_to_all.16 = bf16[32,32,128]{2,1,0:T(8,128)(2,1)S(1)} all-to-all(bf16[32,32,128]{2,1,0:T(8,128)(2,1)S(1)} %sweeps.1), channel_id=1, replica_groups=mesh['energy'=16,'chip'=16,'core'=2] {'chip','core'}, dimensions={0} | all-to-all | bytes 524288 | tf_op jit(solution)/shard_map/all_to_all | solution.py:365
  56.4 0.0 copy-done.1
  56.4 0.0 copy-done.2
  56.4 0.0 copy-done.3
  56.4 0.0 copy-done.4
  56.4 0.0 copy-done
  56.4 1.1 %finish.1 = bf16[16,16,256]{2,1,0:T(8,128)(2,1)S(1)} custom-call(f32[2,256,128]{2,1,0:T(8,128)S(1)} %copy-done.2, bf16[2,256,256]{2,1,0:T(8,128)(2,1)S(1)} %copy-done.1, bf16[2,256,512]{2,1,0:T(8,128)(2,1)S(1)} %copy-done, bf16[32,256]{1,0:T(8,128)(2,1)S(1)} %copy-done.3, bf16[32,256]{1,0:T(8,128)(2,1)S(1)} %copy-done.4, bf16[2,512,128]{2,1,0:T(8,128)(2,1)S(1)} %bitcast.3), custom_call_target="tpu_custom_call" | custom-call | tf_op jit(solution)/shard_map/finish/pallas_call | solution.py:329
  57.6 19.3 %all_to_all.17 = bf16[16,16,256]{2,1,0:T(8,128)(2,1)S(1)} all-to-all(bf16[16,16,256]{2,1,0:T(8,128)(2,1)S(1)} %finish.1), channel_id=1, replica_groups=mesh['energy'=16,'chip'=16,'core'=2] {'energy'}, dimensions={0} | all-to-all | bytes 262144 | tf_op jit(solution)/shard_map/all_to_all | solution.py:376
  76.9 0.6 convert_reduce_fusion
Async XLA Ops:
  32.1 3.8 %collective-permute-start = (bf16[16,128,128]{2,1,0:T(8,128)(2,1)S(1)}, bf16[16,128,128]{2,1,0:T(8,128)(2,1)S(1)}, u32[]{:S(2)}, u32[]{:S(2)}) collective-permute-start(bf16[16,128,128]{2,1,0:T(8,128)(2,1)S(1)} %all_to_all.15.mine_ref), channel_id=1, source_target_pairs={{0,1},{1,0},{2,3},{3,2},{4,5},{5,4},{6,7},{7,6},{8,9},{9,8},{10,11... | collective-permute-start | bytes 1572872 | tf_op jit(solution)/shard_map/ppermute | solution.py:362
  35.9 20.5 %copy-start.1 = (bf16[2,256,256]{2,1,0:T(8,128)(2,1)S(1)}, bf16[2,256,256]{2,1,0:T(8,128)(2,1)}, u32[]{:S(2)}) copy-start(bf16[2,256,256]{2,1,0:T(8,128)(2,1)} %p_ref.1) | copy-start | bytes 786436
  35.9 20.5 %copy-start.2 = (f32[2,256,128]{2,1,0:T(8,128)S(1)}, f32[2,256,128]{2,1,0:T(8,128)}, u32[]{:S(2)}) copy-start(f32[2,256,128]{2,1,0:T(8,128)} %get-tuple-element.7.scale_ref) | copy-start | bytes 786436
  35.9 20.5 %copy-start.3 = (bf16[32,256]{1,0:T(8,128)(2,1)S(1)}, bf16[32,256]{1,0:T(8,128)(2,1)}, u32[]{:S(2)}) copy-start(bf16[32,256]{1,0:T(8,128)(2,1)} %l_ref.1) | copy-start | bytes 49156
  35.9 20.5 %copy-start.4 = (bf16[32,256]{1,0:T(8,128)(2,1)S(1)}, bf16[32,256]{1,0:T(8,128)(2,1)}, u32[]{:S(2)}) copy-start(bf16[32,256]{1,0:T(8,128)(2,1)} %r_ref.1) | copy-start | bytes 49156
  40.6 15.8 %copy-start = (bf16[2,256,512]{2,1,0:T(8,128)(2,1)S(1)}, bf16[2,256,512]{2,1,0:T(8,128)(2,1)}, u32[]{:S(2)}) copy-start(bf16[2,256,512]{2,1,0:T(8,128)(2,1)} %b_ref.1) | copy-start | bytes 1572868

commit v3 on v2

--- a/solution.py
+++ b/solution.py
@@ -17,6 +17,20 @@
 
 def mm_nt(a, b):
     return lax.dot_general(a, b, (((1,), (1,)), ((), ())), preferred_element_type=F32)
+
+
+def pack(step, middle):
+    edge = step.shape[0] // 2
+    most = edge * 3 // 4
+    low = [step[edge:, :edge], step[edge:, edge:], middle[edge:, edge:]]
+    rest = jnp.concatenate([v[most:] for v in low], axis=0)
+    return jnp.concatenate(
+        [
+            jnp.concatenate([step[:edge], middle[:edge]], axis=1),
+            jnp.concatenate([v[:most] for v in low] + [rest], axis=1),
+        ],
+        axis=0,
+    )
 
 
 def prepare(
@@ -67,8 +81,8 @@
     for copy in fetch[3:6]:
         copy.wait()
     couple = c_ref[...]
-    chunk = o_ref.shape[1] - 2 * edge
-    each = modes // chunk
+    each = o_ref.shape[0] // count
+    chunk = modes // each
     energies = range(count)
     rim = [jnp.concatenate([p_ref[e, block - edge :], p_ref[e, :edge]], axis=0) for e in energies]
     u = [mm_nt(couple, p_ref[e]) for e in energies]
@@ -80,7 +94,7 @@
     for e in energies:
         rows = mm(jnp.concatenate([rim[e], outer[e]], axis=0), b_ref[e])
         columns = rows.T.astype(BF16)
-        exact = jnp.concatenate([step[e], middle[e]], axis=1)
+        exact = pack(step[e], middle[e])
         left = jnp.zeros_like(exact)
         for k in range(each):
             left += exact
@@ -100,56 +114,78 @@
 SLOTS = 4
 
 
-def sweep_all(core_ref, mine_ref, other_ref, o_ref, wf_ref, wa_ref, wk_ref):
+def sweep_all(core_ref, x_ref, o_ref, wf_ref, wa_ref, wk_ref):
     strips, chunk, _ = o_ref.shape
     edge = LANES // SLOTS
+    most = edge * 3 // 4
     groups = strips // SLOTS
     wide = 2 * LANES
+    last = groups - 1
     core = core_ref[0]
-    skip = 2 * chunk
+    skip = x_ref.shape[0] * chunk
     evens, odds = range(0, groups, 2), range(1, groups, 2)
 
     def strip(s, rows):
-        return jnp.where(core == s % 2, mine_ref[s // 2, rows], other_ref[s // 2, rows])
+        return x_ref[s % 2, s // 2, rows]
 
     at = lax.broadcasted_iota(jnp.int32, (1, 2 * wide), 1)
     source = ((at >> 7) << 5) | (at & 31)
     spread = lax.broadcasted_iota(jnp.int32, (LANES, 2 * wide), 0) == source
     spread = spread.astype(F32).astype(BF16)
-    at = lax.broadcasted_iota(jnp.int32, (wide, 1), 0)
-    source = ((at >> 7) << 5) | (at & 31)
-    spread_t = lax.broadcasted_iota(jnp.int32, (wide, LANES), 1) == source
+    source = (lax.broadcasted_iota(jnp.int32, (LANES, 1), 0) & 31) | 96
+    spread_t = lax.broadcasted_iota(jnp.int32, (LANES, LANES), 1) == source
     spread_t = spread_t.astype(F32).astype(BF16)
-    row_slot = (lax.broadcasted_iota(jnp.int32, (wide, 1), 0) >> 5) & 3
-    lane_slot = (lax.broadcasted_iota(jnp.int32, (1, 2 * wide), 1) >> 5) & 3
-    def stacked(g, turns):
+    row_slot = lax.broadcasted_iota(jnp.int32, (LANES, 1), 0) >> 5
+    lane_slot = (lax.broadcasted_iota(jnp.int32, (1, wide), 1) >> 5) & 3
+
+    def upper(g, turn):
+        rows = slice(skip, skip + edge)
         return jnp.concatenate(
-            [
-                strip(
-                    g + groups * ((j + turns[a]) % SLOTS),
-                    slice(skip + a * edge, skip + (a + 1) * edge),
-                )
-                for a in range(2)
-                for j in range(SLOTS)
-            ],
-            axis=0,
+            [strip(g + groups * ((j + turn) % SLOTS), rows) for j in range(SLOTS)], axis=0
         )
 
-    def matching(turns, lanes):
-        half = lax.broadcasted_iota(jnp.int32, (wide, 1), 0) >> 7
-        slot = row_slot + jnp.where(half == 0, turns[0], turns[1])
-        return (slot & 3) == lane_slot[:, :lanes]
-
-    last = groups - 1
+    def lower(g, turn):
+        rows = slice(skip + edge, skip + edge + most)
+        short = [
+            strip(g + groups * ((j + turn) % SLOTS), rows).astype(F32) for j in range(SLOTS)
+        ]
+        got = mm(jnp.concatenate(short, axis=0).astype(BF16), spread)
+        parts = []
+        for part in range(3):
+            lanes = slice(part * LANES, (part + 1) * LANES)
+            rows = []
+            for j in range(SLOTS):
+                rest = j * most + part * (edge - most)
+                rows.append(got[j * most : (j + 1) * most, lanes])
+                rows.append(got[rest : rest + edge - most, 3 * LANES :])
+            parts.append(jnp.concatenate(rows, axis=0))
+        return parts
+
+    def fit(value, turn):
+        match = ((row_slot + turn) & 3) == lane_slot[:, : value.shape[1]]
+        return jnp.where(match, value, 0.0).astype(BF16)
+
     for g in range(groups):
-        turns = {0: (1, 0), last: (0, -1)}.get(g, (0, 0))
-        back = {0: (0, 1), last: (-1, 0)}.get(g, (0, 0))
-        both = mm(stacked(g, turns), spread)
-        both = jnp.where(matching(turns, 2 * wide), both, 0.0).astype(BF16)
-        wf_ref[g] = both[:, :wide]
-        wk_ref[g] = both[:, wide:]
-        both = mm_nt(spread_t, stacked(g, (0, 0)))
-        wa_ref[g] = jnp.where(matching(back, wide), both, 0.0).astype(BF16)
+        first, second = 1 if g == 0 else 0, -1 if g == last else 0
+        plain = upper(g, 0)
+        high = mm(upper(g, first) if first else plain, spread)
+        low = lower(g, second)
+        wf_ref[g, :LANES] = fit(high[:, :wide], first)
+        wf_ref[g, LANES:, :LANES] = fit(low[0], second)
+        wf_ref[g, LANES:, LANES:] = fit(low[1], second)
+        wk_ref[g, :LANES] = fit(high[:, wide:], first)
+        wk_ref[g, LANES:, :LANES] = fit(mm_nt(spread_t, plain), second)
+        wk_ref[g, LANES:, LANES:] = fit(low[2], second)
+        if first or second:
+            if first:
+                high = mm(plain, spread)
+            if second:
+                low = lower(g, 0)
+            at = 0 if first else 1
+            wa_ref[at, :LANES, :LANES] = fit(high[:, :LANES], -second)
+            wa_ref[at, :LANES, LANES:] = fit(high[:, LANES:wide], -first)
+            wa_ref[at, LANES:, :LANES] = fit(low[0], -second)
+            wa_ref[at, LANES:, LANES:] = fit(low[1], -first)
 
     at = lax.broadcasted_iota(jnp.int32, (1, 2 * wide), 1)
     source = (((at >> 5) & 3) << 7) | ((at >> 7) << 5) | (at & 31)
@@ -190,11 +226,11 @@
         parts[last] = turn(parts[last], 1 if first_up else 0, LANES - edge)
         return parts
 
-    def iterate(base, weights, first_up):
+    def iterate(base, step, first_up):
         even, odd = [base[g] for g in evens], [base[g] for g in odds]
         ahead, behind = odd, even
         z = arrive(ahead, 1, first_up)
-        ahead = [even[i] + mm(z[i], weights[g]) for i, g in enumerate(evens)]
+        ahead = [even[i] + step(z[i], g) for i, g in enumerate(evens)]
         for t in range(1, SWEEPS - 2):
             at = (t + 1) % 2
             z = arrive(ahead, at, first_up)
@@ -202,14 +238,14 @@
             add = odd if at == 0 else even
             both = []
             for i, g in enumerate(odds if at == 0 else evens):
-                both.append(mm(jnp.concatenate([z[i], y[i]], axis=0), weights[g]))
+                both.append(step(jnp.concatenate([z[i], y[i]], axis=0), g))
             ahead = [add[i] + v[:chunk] for i, v in enumerate(both)]
             behind = [add[i] + v[chunk:] for i, v in enumerate(both)]
         at = (SWEEPS - 1) % 2
         y = arrive(behind, at, first_up)
         add = odd if at == 0 else even
         behind = [
-            add[i] + mm(y[i], weights[g]) for i, g in enumerate(odds if at == 0 else evens)
+            add[i] + step(y[i], g) for i, g in enumerate(odds if at == 0 else evens)
         ]
         gets_ahead, gets_behind = arrive(ahead, at, first_up), arrive(behind, 1 - at, first_up)
         got = [None] * groups
@@ -220,11 +256,12 @@
         return got
 
     base = [start[g * chunk : (g + 1) * chunk, :wide] for g in range(groups)]
-    z = iterate(base, wf_ref, True)
+    z = iterate(base, lambda v, g: mm(v, wf_ref[g]), True)
     base = [
         start[g * chunk : (g + 1) * chunk, wide:] + mm(z[g], wk_ref[g]) for g in range(groups)
     ]
-    y = iterate(base, wa_ref, False)
+    ends = {0: wa_ref.at[0], last: wa_ref.at[1]}
+    y = iterate(base, lambda v, g: mm_nt(v, ends[g][...] if g in ends else wf_ref[g]), False)
     z, y = turned(z, True), turned(y, False)
     out = jnp.concatenate(
         [jnp.concatenate([z[g], y[g]], axis=1) for g in range(groups)], axis=0
@@ -287,7 +324,7 @@
 def call_prepare(scalars, inverse, source, left, right, chips, cores, chunk):
     count, block, modes = source.shape
     edge = left.shape[0]
-    pieces = (chips, cores * chunk + 2 * edge, 4 * edge)
+    pieces = (chips, cores * chunk + edge + edge * 3 // 4, 4 * edge)
     return pl.pallas_call(
         prepare,
         out_shape=(shape(pieces, BF16), shape((count, block, LANES), F32)),
@@ -308,20 +345,23 @@
     )(*scalars, inverse, source, left, right)
 
 
-def call_sweeps(core, mine, other):
-    chips, rows, lanes = mine.shape
-    strips = 2 * chips
-    chunk = (rows - 2 * lanes // SLOTS) // 2
-    weights = pltpu.VMEM((strips // SLOTS, 2 * LANES, 2 * LANES), BF16)
+def call_sweeps(core, given, chunk):
+    cores, chips, _, lanes = given.shape
+    strips = cores * chips
+    weights = (strips // SLOTS, 2 * LANES, 2 * LANES)
     return pl.pallas_call(
         sweep_all,
         out_shape=shape((strips, chunk, lanes), BF16),
-        in_specs=[SMEM] + [VMEM] * 2,
+        in_specs=[SMEM, VMEM],
         out_specs=VMEM,
-        scratch_shapes=[weights] * 3,
+        scratch_shapes=[
+            pltpu.VMEM(weights, BF16),
+            pltpu.VMEM((2,) + weights[1:], BF16),
+            pltpu.VMEM(weights, BF16),
+        ],
         name="sweeps",
         **PARAMS,
-    )(core, mine, other)
+    )(core, given)
 
 
 def call_finish(scale, inverse, source, left, right, columns, energies, owned):
@@ -359,9 +399,9 @@
         scalars, inverse_blocks, source, left_coupling, right_coupling, chips, cores, chunk
     )
     mine = lax.all_to_all(pieces, "chip", 0, 0, tiled=True)
-    other = lax.ppermute(mine, "core", [(i, cores - 1 - i) for i in range(cores)])
+    given = lax.all_gather(mine, "core")
     core = lax.axis_index("core").astype(jnp.int32).reshape(1)
-    out = call_sweeps(core, mine, other)
+    out = call_sweeps(core, given, chunk)
     out = lax.all_to_all(out, ("chip", "core"), 0, 0, tiled=True)
     out = call_finish(
         scale,

time: 77.8 us -> 75.9 us (0.976)
  blocking collectives: 63.4 us -> 37.5 us
  waiting for transfers between devices: 1.87 us -> 15.8 us
  starting transfers between devices: 1.91 us -> 11.8 us
    all_to_all x1 -> x0, blocking collectives: 28.3 us -> none  [body(): mine = lax.all_to_all(pieces, 'chip', 0, 0, tiled=True)]
    all_to_all x0 -> x1, waiting for transfers between devices: none -> 15.8 us  [body(): mine = lax.all_to_all(pieces, 'chip', 0, 0, tiled=True)]
    all_to_all x0 -> x1, starting transfers between devices: none -> 11.8 us  [body(): mine = lax.all_to_all(pieces, 'chip', 0, 0, tiled=True)]
    all_gather x0 -> x1, blocking collectives: none -> 2.5 us  [body(): given = lax.all_gather(mine, 'core')]
    ppermute x1 -> x0, starting transfers between devices: 1.91 us -> none  [body(): lax.ppermute(mine, 'core', [(i, cores - 1 - i) for i in range(cores)])]
    ppermute x1 -> x0, waiting for transfers between devices: 1.87 us -> none  [body(): lax.ppermute(mine, 'core', [(i, cores - 1 - i) for i in range(cores)])]
where the time goes in v3:
time: 75.9 us; the launch traced here: 75.6 us
  blocking collectives  37.5 us (49%)
  waiting for transfers between devices  15.8 us (21%)
  starting transfers between devices  11.8 us (16%)
  Pallas kernels  8.41 us (11%)
  between operations  1.36 us (2%)
    all_to_all x1, blocking collectives, body(): out = lax.all_to_all(out, 'energy', 0, 0, tiled=True)  19.3 us
    all_to_all x1, waiting for transfers between devices, body(): mine = lax.all_to_all(pieces, 'chip', 0, 0, tiled=True)  15.8 us
    all_to_all x1, blocking collectives, body(): out = lax.all_to_all(out, ('chip', 'core'), 0, 0, tiled=True)  15.7 us
    all_to_all x1, starting transfers between devices, body(): mine = lax.all_to_all(pieces, 'chip', 0, 0, tiled=True)  11.8 us
    pallas_call x1, Pallas kernels, call_sweeps(): pl.pallas_call(sweep_all, out_shape=shape((strips, chunk, lanes), BF16),...  4.78 us
    pallas_call x1, Pallas kernels, call_prepare(): pl.pallas_call(prepare, out_shape=(shape(pieces, BF16), shape((count, blo...  2.5 us
    all_gather x1, blocking collectives, body(): given = lax.all_gather(mine, 'core')  2.5 us
  transfers between devices with their start and end apart: 1, of which 1 were waited for; matrix products, arithmetic and copies ran while one was open for 0% of the time, Pallas kernels for 0%

profile of v3, /device:TPU:8, one launch (start us, length us, event | category | flops | bytes accessed | tf_op | source)
XLA Modules:
  0.0 75.6 jit_solution(9729311016328368063)
XLA Ops:
  1.3 2.5 %prepare.1 = (bf16[16,120,128]{2,1,0:T(8,128)(2,1)}, f32[2,256,128]{2,1,0:T(8,128)}) custom-call(f32[2]{0:T(128)} %w_hbm.1, s32[1]{0:T(128)S(6)} %copy.8.low_hbm, s32[1]{0:T(128)S(6)} %copy.9.high_hbm, bf16[2,256,256]{2,1,0:T(8,128)(2,1)} %p_ref.1, bf16[2,256,512]{2,1,0:T(8,128)(2,1)} %b_ref.1, bf16[32,256]{1,0:T(8,128)(2,1)} %l_ref.1, bf16[32,256]{1,0:T(8,128)(2,1)} %r_ref.1), custom_call_target="tpu_custom_call" | custom-call | tf_op jit(solution)/shard_map/prepare/pallas_call | solution.py:328
  3.8 11.8 %all-to-all-start = ((bf16[16,120,128]{2,1,0:T(8,128)(2,1)}), bf16[16,120,128]{2,1,0:T(8,128)(2,1)S(1)}, u32[]{:S(2)}, u32[]{:S(2)}) async-start(bf16[16,120,128]{2,1,0:T(8,128)(2,1)} %get-tuple-element.8), calls=%async_computation | async-start | bytes 983040 | tf_op jit(solution)/shard_map/all_to_all | solution.py:401
  15.6 15.8 %all-to-all-done = bf16[16,120,128]{2,1,0:T(8,128)(2,1)S(1)} async-done(((bf16[16,120,128]{2,1,0:T(8,128)(2,1)}), bf16[16,120,128]{2,1,0:T(8,128)(2,1)S(1)}, u32[]{:S(2)}, u32[]{:S(2)}) %all-to-all-start) | async-done | bytes 491552 | tf_op jit(solution)/shard_map/all_to_all | solution.py:401
  31.5 2.5 %all-gather = bf16[32,120,128]{2,1,0:T(8,128)(2,1)S(1)} all-gather(bf16[16,120,128]{2,1,0:T(8,128)(2,1)S(1)} %all-to-all-done), channel_id=2, replica_groups=mesh['energy'=16,'chip'=16,'core'=2] {'core'}, dimensions={0}, use_global_device_ids=true | all-gather | bytes 1474560 | tf_op jit(solution)/shard_map/all_gather | solution.py:402
  34.0 0.0 copy-start.1
  34.0 0.0 copy-start.2
  34.0 0.0 copy-start.3
  34.0 0.0 copy-start.4
  34.0 4.8 %sweeps.1 = bf16[32,32,128]{2,1,0:T(8,128)(2,1)S(1)} custom-call(s32[1]{0:T(128)} %bitcast.core_ref, bf16[2,16,120,128]{3,2,1,0:T(8,128)(2,1)S(1)} %bitcast.4), custom_call_target="tpu_custom_call" | custom-call | tf_op jit(solution)/shard_map/sweeps/pallas_call | solution.py:352
  38.7 0.0 copy-start
  38.8 15.7 %all_to_all.15 = bf16[32,32,128]{2,1,0:T(8,128)(2,1)S(1)} all-to-all(bf16[32,32,128]{2,1,0:T(8,128)(2,1)S(1)} %sweeps.1), channel_id=1, replica_groups=mesh['energy'=16,'chip'=16,'core'=2] {'chip','core'}, dimensions={0} | all-to-all | bytes 524288 | tf_op jit(solution)/shard_map/all_to_all | solution.py:405
  54.5 0.0 copy-done.1
  54.5 0.0 copy-done.2
  54.5 0.0 copy-done.3
  54.5 0.0 copy-done.4
  54.5 0.0 copy-done
  54.5 1.1 %finish.1 = bf16[16,16,256]{2,1,0:T(8,128)(2,1)S(1)} custom-call(f32[2,256,128]{2,1,0:T(8,128)S(1)} %copy-done.2, bf16[2,256,256]{2,1,0:T(8,128)(2,1)S(1)} %copy-done.1, bf16[2,256,512]{2,1,0:T(8,128)(2,1)S(1)} %copy-done, bf16[32,256]{1,0:T(8,128)(2,1)S(1)} %copy-done.3, bf16[32,256]{1,0:T(8,128)(2,1)S(1)} %copy-done.4, bf16[2,512,128]{2,1,0:T(8,128)(2,1)S(1)} %bitcast.5), custom_call_target="tpu_custom_call" | custom-call | tf_op jit(solution)/shard_map/finish/pallas_call | solution.py:369
  55.7 19.3 %all_to_all.16 = bf16[16,16,256]{2,1,0:T(8,128)(2,1)S(1)} all-to-all(bf16[16,16,256]{2,1,0:T(8,128)(2,1)S(1)} %finish.1), channel_id=1, replica_groups=mesh['energy'=16,'chip'=16,'core'=2] {'energy'}, dimensions={0} | all-to-all | bytes 262144 | tf_op jit(solution)/shard_map/all_to_all | solution.py:416
  75.0 0.6 convert_reduce_fusion
Async XLA Ops:
  3.8 27.7 %all-to-all-start = ((bf16[16,120,128]{2,1,0:T(8,128)(2,1)}), bf16[16,120,128]{2,1,0:T(8,128)(2,1)S(1)}, u32[]{:S(2)}, u32[]{:S(2)}) async-start(bf16[16,120,128]{2,1,0:T(8,128)(2,1)} %get-tuple-element.8), calls=%async_computation | async-start | bytes 983040 | tf_op jit(solution)/shard_map/all_to_all | solution.py:401
  34.0 20.5 %copy-start.1 = (bf16[2,256,256]{2,1,0:T(8,128)(2,1)S(1)}, bf16[2,256,256]{2,1,0:T(8,128)(2,1)}, u32[]{:S(2)}) copy-start(bf16[2,256,256]{2,1,0:T(8,128)(2,1)} %p_ref.1) | copy-start | bytes 786436
  34.0 20.5 %copy-start.2 = (f32[2,256,128]{2,1,0:T(8,128)S(1)}, f32[2,256,128]{2,1,0:T(8,128)}, u32[]{:S(2)}) copy-start(f32[2,256,128]{2,1,0:T(8,128)} %get-tuple-element.7.scale_ref) | copy-start | bytes 786436
  34.0 20.5 %copy-start.3 = (bf16[32,256]{1,0:T(8,128)(2,1)S(1)}, bf16[32,256]{1,0:T(8,128)(2,1)}, u32[]{:S(2)}) copy-start(bf16[32,256]{1,0:T(8,128)(2,1)} %l_ref.1) | copy-start | bytes 49156
  34.0 20.5 %copy-start.4 = (bf16[32,256]{1,0:T(8,128)(2,1)S(1)}, bf16[32,256]{1,0:T(8,128)(2,1)}, u32[]{:S(2)}) copy-start(bf16[32,256]{1,0:T(8,128)(2,1)} %r_ref.1) | copy-start | bytes 49156
  38.7 15.8 %copy-start = (bf16[2,256,512]{2,1,0:T(8,128)(2,1)S(1)}, bf16[2,256,512]{2,1,0:T(8,128)(2,1)}, u32[]{:S(2)}) copy-start(bf16[2,256,512]{2,1,0:T(8,128)(2,1)} %b_ref.1) | copy-start | bytes 1572868

commit v4 on v3

--- a/solution.py
+++ b/solution.py
@@ -115,14 +115,15 @@
 
 
 def sweep_all(core_ref, x_ref, o_ref, wf_ref, wa_ref, wk_ref):
-    strips, chunk, _ = o_ref.shape
+    chips, chunk, _ = o_ref.shape
+    strips = chips * x_ref.shape[0]
     edge = LANES // SLOTS
     most = edge * 3 // 4
     groups = strips // SLOTS
     wide = 2 * LANES
     last = groups - 1
     core = core_ref[0]
-    skip = x_ref.shape[0] * chunk
+    skip = chunk
     evens, odds = range(0, groups, 2), range(1, groups, 2)
 
     def strip(s, rows):
@@ -191,10 +192,9 @@
     source = (((at >> 5) & 3) << 7) | ((at >> 7) << 5) | (at & 31)
     order = lax.broadcasted_iota(jnp.int32, (2 * wide, 2 * wide), 0) == source
     order = order.astype(F32).astype(BF16)
-    mine = pl.ds(pl.multiple_of(core * chunk, chunk), chunk)
     start = jnp.concatenate(
         [
-            jnp.concatenate([strip(g + groups * j, mine) for j in range(SLOTS)], axis=1)
+            jnp.concatenate([strip(g + groups * j, slice(chunk)) for j in range(SLOTS)], axis=1)
             for g in range(groups)
         ],
         axis=0,
@@ -262,14 +262,14 @@
     ]
     ends = {0: wa_ref.at[0], last: wa_ref.at[1]}
     y = iterate(base, lambda v, g: mm_nt(v, ends[g][...] if g in ends else wf_ref[g]), False)
-    z, y = turned(z, True), turned(y, False)
-    out = jnp.concatenate(
-        [jnp.concatenate([z[g], y[g]], axis=1) for g in range(groups)], axis=0
-    )
-    out = mm(out, order).astype(BF16)
-    for g in range(groups):
+    out = [jnp.concatenate(v, axis=1) for v in zip(turned(z, True), turned(y, False))]
+    out = [jnp.where(core == 0, out[g], out[g + 1]) for g in evens]
+    out = mm(jnp.concatenate(out, axis=0), order).astype(BF16)
+    for i, g in enumerate(evens):
         for j in range(SLOTS):
-            o_ref[g + groups * j] = out[g * chunk : (g + 1) * chunk, j * LANES : (j + 1) * LANES]
+            o_ref[(g + groups * j) // 2] = out[
+                i * chunk : (i + 1) * chunk, j * LANES : (j + 1) * LANES
+            ]
 
 
 def finish(scale_ref, p_ref, b_ref, l_ref, r_ref, zy_ref, o_ref):
@@ -321,10 +321,10 @@
 shape = jax.ShapeDtypeStruct
 
 
-def call_prepare(scalars, inverse, source, left, right, chips, cores, chunk):
+def call_prepare(scalars, inverse, source, left, right, chips):
     count, block, modes = source.shape
     edge = left.shape[0]
-    pieces = (chips, cores * chunk + edge + edge * 3 // 4, 4 * edge)
+    pieces = (chips, count * modes // chips + edge + edge * 3 // 4, 4 * edge)
     return pl.pallas_call(
         prepare,
         out_shape=(shape(pieces, BF16), shape((count, block, LANES), F32)),
@@ -347,11 +347,10 @@
 
 def call_sweeps(core, given, chunk):
     cores, chips, _, lanes = given.shape
-    strips = cores * chips
-    weights = (strips // SLOTS, 2 * LANES, 2 * LANES)
+    weights = (cores * chips // SLOTS, 2 * LANES, 2 * LANES)
     return pl.pallas_call(
         sweep_all,
-        out_shape=shape((strips, chunk, lanes), BF16),
+        out_shape=shape((chips, chunk, lanes), BF16),
         in_specs=[SMEM, VMEM],
         out_specs=VMEM,
         scratch_shapes=[
@@ -388,21 +387,19 @@
     count, block, modes = source.shape
     edge = left_coupling.shape[0]
     chips = lax.axis_size("chip")
-    cores = lax.axis_size("core")
-    strips = chips * cores
     energies = lax.axis_size("energy")
-    chunk = count * modes // strips
+    chunk = count * modes // chips
     owned = block // energies
     scalars = (energy_weights, collector_low, collector_high)
 
     pieces, scale = call_prepare(
-        scalars, inverse_blocks, source, left_coupling, right_coupling, chips, cores, chunk
+        scalars, inverse_blocks, source, left_coupling, right_coupling, chips
     )
     mine = lax.all_to_all(pieces, "chip", 0, 0, tiled=True)
     given = lax.all_gather(mine, "core")
     core = lax.axis_index("core").astype(jnp.int32).reshape(1)
     out = call_sweeps(core, given, chunk)
-    out = lax.all_to_all(out, ("chip", "core"), 0, 0, tiled=True)
+    out = lax.all_to_all(out, "chip", 0, 0, tiled=True)
     out = call_finish(
         scale,
         inverse_blocks,

time: 75.9 us -> 74.6 us (0.983)
  blocking collectives: 37.5 us -> 36.1 us
    all_to_all x1, blocking collectives: 15.7 us -> 14.3 us  [body(): out = lax.all_to_all(out, 'chip', 0, 0, tiled=True)]
where the time goes in v4:
time: 74.6 us; the launch traced here: 74.3 us
  blocking collectives  36.1 us (48%)
  waiting for transfers between devices  15.8 us (21%)
  starting transfers between devices  11.8 us (16%)
  Pallas kernels  8.61 us (12%)
  between operations  1.36 us (2%)
    all_to_all x1, blocking collectives, body(): out = lax.all_to_all(out, 'energy', 0, 0, tiled=True)  19.2 us
    all_to_all x1, waiting for transfers between devices, body(): mine = lax.all_to_all(pieces, 'chip', 0, 0, tiled=True)  15.8 us
    all_to_all x1, blocking collectives, body(): out = lax.all_to_all(out, 'chip', 0, 0, tiled=True)  14.3 us
    all_to_all x1, starting transfers between devices, body(): mine = lax.all_to_all(pieces, 'chip', 0, 0, tiled=True)  11.8 us
    pallas_call x1, Pallas kernels, call_sweeps(): pl.pallas_call(sweep_all, out_shape=shape((chips, chunk, lanes), BF16), i...  4.98 us
    pallas_call x1, Pallas kernels, call_prepare(): pl.pallas_call(prepare, out_shape=(shape(pieces, BF16), shape((count, blo...  2.5 us
    all_gather x1, blocking collectives, body(): given = lax.all_gather(mine, 'core')  2.5 us
  transfers between devices with their start and end apart: 1, of which 1 were waited for; matrix products, arithmetic and copies ran while one was open for 0% of the time, Pallas kernels for 0%

profile of v4, /device:TPU:8, one launch (start us, length us, event | category | flops | bytes accessed | tf_op | source)
XLA Modules:
  0.0 74.3 jit_solution(6782788428532105073)
XLA Ops:
  1.3 2.5 %prepare.1 = (bf16[16,120,128]{2,1,0:T(8,128)(2,1)}, f32[2,256,128]{2,1,0:T(8,128)}) custom-call(f32[2]{0:T(128)} %w_hbm.1, s32[1]{0:T(128)S(6)} %copy.8.low_hbm, s32[1]{0:T(128)S(6)} %copy.9.high_hbm, bf16[2,256,256]{2,1,0:T(8,128)(2,1)} %p_ref.1, bf16[2,256,512]{2,1,0:T(8,128)(2,1)} %b_ref.1, bf16[32,256]{1,0:T(8,128)(2,1)} %l_ref.1, bf16[32,256]{1,0:T(8,128)(2,1)} %r_ref.1), custom_call_target="tpu_custom_call" | custom-call | tf_op jit(solution)/shard_map/prepare/pallas_call | solution.py:328
  3.8 11.8 %all-to-all-start = ((bf16[16,120,128]{2,1,0:T(8,128)(2,1)}), bf16[16,120,128]{2,1,0:T(8,128)(2,1)S(1)}, u32[]{:S(2)}, u32[]{:S(2)}) async-start(bf16[16,120,128]{2,1,0:T(8,128)(2,1)} %get-tuple-element.8), calls=%async_computation | async-start | bytes 983040 | tf_op jit(solution)/shard_map/all_to_all | solution.py:398
  15.6 15.8 %all-to-all-done = bf16[16,120,128]{2,1,0:T(8,128)(2,1)S(1)} async-done(((bf16[16,120,128]{2,1,0:T(8,128)(2,1)}), bf16[16,120,128]{2,1,0:T(8,128)(2,1)S(1)}, u32[]{:S(2)}, u32[]{:S(2)}) %all-to-all-start) | async-done | bytes 491552 | tf_op jit(solution)/shard_map/all_to_all | solution.py:398
  31.5 2.5 %all-gather = bf16[32,120,128]{2,1,0:T(8,128)(2,1)S(1)} all-gather(bf16[16,120,128]{2,1,0:T(8,128)(2,1)S(1)} %all-to-all-done), channel_id=2, replica_groups=mesh['energy'=16,'chip'=16,'core'=2] {'core'}, dimensions={0}, use_global_device_ids=true | all-gather | bytes 1474560 | tf_op jit(solution)/shard_map/all_gather | solution.py:399
  34.0 0.0 copy-start.1
  34.0 0.0 copy-start.2
  34.0 0.0 copy-start.3
  34.0 0.0 copy-start.4
  34.0 5.0 %sweeps.1 = bf16[16,64,128]{2,1,0:T(8,128)(2,1)S(1)} custom-call(s32[1]{0:T(128)} %bitcast.core_ref, bf16[2,16,120,128]{3,2,1,0:T(8,128)(2,1)S(1)} %bitcast.4), custom_call_target="tpu_custom_call" | custom-call | tf_op jit(solution)/shard_map/sweeps/pallas_call | solution.py:351
  38.9 0.0 copy-start
  39.0 14.3 %all_to_all.15 = bf16[16,64,128]{2,1,0:T(8,128)(2,1)S(1)} all-to-all(bf16[16,64,128]{2,1,0:T(8,128)(2,1)S(1)} %sweeps.1), channel_id=1, replica_groups=mesh['energy'=16,'chip'=16,'core'=2] {'chip'}, dimensions={0} | all-to-all | bytes 524288 | tf_op jit(solution)/shard_map/all_to_all | solution.py:402
  53.3 0.0 copy-done.1
  53.3 0.0 copy-done.2
  53.3 0.0 copy-done.3
  53.3 0.0 copy-done.4
  53.3 0.0 copy-done
  53.3 1.1 %finish.1 = bf16[16,16,256]{2,1,0:T(8,128)(2,1)S(1)} custom-call(f32[2,256,128]{2,1,0:T(8,128)S(1)} %copy-done.2, bf16[2,256,256]{2,1,0:T(8,128)(2,1)S(1)} %copy-done.1, bf16[2,256,512]{2,1,0:T(8,128)(2,1)S(1)} %copy-done, bf16[32,256]{1,0:T(8,128)(2,1)S(1)} %copy-done.3, bf16[32,256]{1,0:T(8,128)(2,1)S(1)} %copy-done.4, bf16[2,512,128]{2,1,0:T(8,128)(2,1)S(1)} %bitcast.5), custom_call_target="tpu_custom_call" | custom-call | tf_op jit(solution)/shard_map/finish/pallas_call | solution.py:368
  54.5 19.2 %all_to_all.16 = bf16[16,16,256]{2,1,0:T(8,128)(2,1)S(1)} all-to-all(bf16[16,16,256]{2,1,0:T(8,128)(2,1)S(1)} %finish.1), channel_id=1, replica_groups=mesh['energy'=16,'chip'=16,'core'=2] {'energy'}, dimensions={0} | all-to-all | bytes 262144 | tf_op jit(solution)/shard_map/all_to_all | solution.py:413
  73.7 0.6 convert_reduce_fusion
Async XLA Ops:
  3.8 27.7 %all-to-all-start = ((bf16[16,120,128]{2,1,0:T(8,128)(2,1)}), bf16[16,120,128]{2,1,0:T(8,128)(2,1)S(1)}, u32[]{:S(2)}, u32[]{:S(2)}) async-start(bf16[16,120,128]{2,1,0:T(8,128)(2,1)} %get-tuple-element.8), calls=%async_computation | async-start | bytes 983040 | tf_op jit(solution)/shard_map/all_to_all | solution.py:398
  34.0 19.4 %copy-start.1 = (bf16[2,256,256]{2,1,0:T(8,128)(2,1)S(1)}, bf16[2,256,256]{2,1,0:T(8,128)(2,1)}, u32[]{:S(2)}) copy-start(bf16[2,256,256]{2,1,0:T(8,128)(2,1)} %p_ref.1) | copy-start | bytes 786436
  34.0 19.4 %copy-start.2 = (f32[2,256,128]{2,1,0:T(8,128)S(1)}, f32[2,256,128]{2,1,0:T(8,128)}, u32[]{:S(2)}) copy-start(f32[2,256,128]{2,1,0:T(8,128)} %get-tuple-element.7.scale_ref) | copy-start | bytes 786436
  34.0 19.4 %copy-start.3 = (bf16[32,256]{1,0:T(8,128)(2,1)S(1)}, bf16[32,256]{1,0:T(8,128)(2,1)}, u32[]{:S(2)}) copy-start(bf16[32,256]{1,0:T(8,128)(2,1)} %l_ref.1) | copy-start | bytes 49156
  34.0 19.4 %copy-start.4 = (bf16[32,256]{1,0:T(8,128)(2,1)S(1)}, bf16[32,256]{1,0:T(8,128)(2,1)}, u32[]{:S(2)}) copy-start(bf16[32,256]{1,0:T(8,128)(2,1)} %r_ref.1) | copy-start | bytes 49156
  38.9 14.4 %copy-start = (bf16[2,256,512]{2,1,0:T(8,128)(2,1)S(1)}, bf16[2,256,512]{2,1,0:T(8,128)(2,1)}, u32[]{:S(2)}) copy-start(bf16[2,256,512]{2,1,0:T(8,128)(2,1)} %b_ref.1) | copy-start | bytes 1572868

commit v5 on v4

--- a/solution.py
+++ b/solution.py
@@ -35,30 +35,24 @@
 
 def prepare(
     w_hbm,
-    low_hbm,
-    high_hbm,
+    low_ref,
+    high_ref,
     p_hbm,
     b_hbm,
     l_hbm,
     r_hbm,
-    o_hbm,
-    scale_hbm,
+    o_ref,
+    scale_ref,
     w_ref,
-    low_ref,
-    high_ref,
     p_ref,
     b_ref,
     c_ref,
-    o_ref,
-    scale_ref,
     sems,
 ):
     count, block, modes = b_ref.shape
     edge = l_hbm.shape[0]
     fetch = [
         (w_hbm, w_ref),
-        (low_hbm, low_ref),
-        (high_hbm, high_ref),
         (l_hbm, c_ref.at[pl.ds(0, edge)]),
         (r_hbm, c_ref.at[pl.ds(edge, edge)]),
         (p_hbm, p_ref),
@@ -67,18 +61,15 @@
     fetch = [pltpu.make_async_copy(*ends, sems.at[i]) for i, ends in enumerate(fetch)]
     for copy in fetch:
         copy.start()
-    for copy in fetch[:3]:
-        copy.wait()
+    fetch[0].wait()
     low, high = low_ref[0], high_ref[0]
     at = lax.broadcasted_iota(jnp.int32, (block, LANES), 0)
     inside = (at >= low) & (at < high)
     for e in range(count):
         scale_ref[e] = jnp.where(inside, 2.0 * w_ref[e], 0.0)
-    keep = [pltpu.make_async_copy(scale_ref, scale_hbm, sems.at[len(fetch)])]
-    keep[0].start()
     at = lax.broadcasted_iota(jnp.int32, (1, block), 1)
     inside = (at >= low) & (at < high)
-    for copy in fetch[3:6]:
+    for copy in fetch[1:4]:
         copy.wait()
     couple = c_ref[...]
     each = o_ref.shape[0] // count
@@ -90,7 +81,7 @@
     weighted = [jnp.where(inside, u[e] * (2.0 * w_ref[e]), 0.0).astype(BF16) for e in energies]
     outer = [mm(weighted[e], p_ref[e]).astype(BF16) for e in energies]
     middle = [mm_nt(weighted[e], u[e].astype(BF16)) for e in energies]
-    fetch[6].wait()
+    fetch[4].wait()
     for e in energies:
         rows = mm(jnp.concatenate([rim[e], outer[e]], axis=0), b_ref[e])
         columns = rows.T.astype(BF16)
@@ -102,19 +93,12 @@
             left -= rounded.astype(F32)
             o_ref[e * each + k, chunk:] = rounded
             o_ref[e * each + k, :chunk] = columns[k * chunk : (k + 1) * chunk]
-        part = pl.ds(e * each, each)
-        keep.append(
-            pltpu.make_async_copy(o_ref.at[part], o_hbm.at[part], sems.at[len(fetch) + 1 + e])
-        )
-        keep[-1].start()
-    for copy in keep:
-        copy.wait()
 
 
 SLOTS = 4
 
 
-def sweep_all(core_ref, x_ref, o_ref, wf_ref, wa_ref, wk_ref):
+def sweep_all(x_ref, o_ref, wf_ref, wa_ref, wk_ref):
     chips, chunk, _ = o_ref.shape
     strips = chips * x_ref.shape[0]
     edge = LANES // SLOTS
@@ -122,7 +106,7 @@
     groups = strips // SLOTS
     wide = 2 * LANES
     last = groups - 1
-    core = core_ref[0]
+    core = lax.axis_index("core")
     skip = chunk
     evens, odds = range(0, groups, 2), range(1, groups, 2)
 
@@ -324,34 +308,35 @@
 def call_prepare(scalars, inverse, source, left, right, chips):
     count, block, modes = source.shape
     edge = left.shape[0]
+    held = [pltpu.with_memory_space_constraint(scalars[0], pltpu.HBM)]
+    tensors = [
+        pltpu.with_memory_space_constraint(v, pltpu.HBM) for v in (inverse, source, left, right)
+    ]
     pieces = (chips, count * modes // chips + edge + edge * 3 // 4, 4 * edge)
     return pl.pallas_call(
         prepare,
-        out_shape=(shape(pieces, BF16), shape((count, block, LANES), F32)),
-        in_specs=[ANY] * 7,
-        out_specs=(ANY, ANY),
+        out_shape=(pltpu.VMEM(pieces, BF16), pltpu.VMEM((count, block, LANES), F32)),
+        in_specs=[ANY, SMEM, SMEM] + [ANY] * 4,
+        out_specs=(VMEM, VMEM),
         scratch_shapes=[
             pltpu.SMEM((count,), F32),
-            pltpu.SMEM((1,), jnp.int32),
-            pltpu.SMEM((1,), jnp.int32),
             pltpu.VMEM((count, block, block), BF16),
             pltpu.VMEM((count, block, modes), BF16),
             pltpu.VMEM((2 * edge, block), BF16),
-            pltpu.VMEM(pieces, BF16),
-            pltpu.VMEM((count, block, LANES), F32),
-            pltpu.SemaphoreType.DMA((8 + count,)),
+            pltpu.SemaphoreType.DMA((5,)),
         ],
         name="prepare",
-    )(*scalars, inverse, source, left, right)
-
-
-def call_sweeps(core, given, chunk):
+        **PARAMS,
+    )(*held, *scalars[1:], *tensors)
+
+
+def call_sweeps(given, chunk):
     cores, chips, _, lanes = given.shape
     weights = (cores * chips // SLOTS, 2 * LANES, 2 * LANES)
     return pl.pallas_call(
         sweep_all,
         out_shape=shape((chips, chunk, lanes), BF16),
-        in_specs=[SMEM, VMEM],
+        in_specs=[VMEM],
         out_specs=VMEM,
         scratch_shapes=[
             pltpu.VMEM(weights, BF16),
@@ -360,7 +345,7 @@
         ],
         name="sweeps",
         **PARAMS,
-    )(core, given)
+    )(given)
 
 
 def call_finish(scale, inverse, source, left, right, columns, energies, owned):
@@ -397,8 +382,7 @@
     )
     mine = lax.all_to_all(pieces, "chip", 0, 0, tiled=True)
     given = lax.all_gather(mine, "core")
-    core = lax.axis_index("core").astype(jnp.int32).reshape(1)
-    out = call_sweeps(core, given, chunk)
+    out = call_sweeps(given, chunk)
     out = lax.all_to_all(out, "chip", 0, 0, tiled=True)
     out = call_finish(
         scale,

time: 74.6 us -> 73.6 us (0.987)
  blocking collectives: 36.1 us -> 63.5 us
  waiting for transfers between devices: 15.8 us -> 0 us
  starting transfers between devices: 11.8 us -> 0 us
  Pallas kernels: 8.61 us -> 7.81 us
    all_to_all x0 -> x1, blocking collectives: none -> 27.4 us  [body(): mine = lax.all_to_all(pieces, 'chip', 0, 0, tiled=True)]
    all_to_all x1 -> x0, waiting for transfers between devices: 15.8 us -> none  [body(): mine = lax.all_to_all(pieces, 'chip', 0, 0, tiled=True)]
    all_to_all x1 -> x0, starting transfers between devices: 11.8 us -> none  [body(): mine = lax.all_to_all(pieces, 'chip', 0, 0, tiled=True)]
    pallas_call x1, Pallas kernels: 2.5 us -> 1.71 us  [call_prepare(): pl.pallas_call(prepare, out_shape=(pltpu.VMEM(pieces, BF16), pltpu.VMEM((...]
  transfers between devices with their start and end apart: 1 -> 0, of which waited for: 1 -> 0; matrix products, arithmetic and copies ran while one was open for 0% -> 0% of each run, Pallas kernels for 0% -> 0%
where the time goes in v5:
time: 73.6 us; the launch traced here: 73.3 us
  blocking collectives  63.5 us (86%)
  Pallas kernels  7.81 us (11%)
  between operations  1.34 us (2%)
    all_to_all x1, blocking collectives, body(): mine = lax.all_to_all(pieces, 'chip', 0, 0, tiled=True)  27.4 us
    all_to_all x1, blocking collectives, body(): out = lax.all_to_all(out, 'energy', 0, 0, tiled=True)  19.2 us
    all_to_all x1, blocking collectives, body(): out = lax.all_to_all(out, 'chip', 0, 0, tiled=True)  14.3 us
    pallas_call x1, Pallas kernels, call_sweeps(): pl.pallas_call(sweep_all, out_shape=shape((chips, chunk, lanes), BF16), i...  4.97 us
    all_gather x1, blocking collectives, body(): given = lax.all_gather(mine, 'core')  2.5 us
    pallas_call x1, Pallas kernels, call_prepare(): pl.pallas_call(prepare, out_shape=(pltpu.VMEM(pieces, BF16), pltpu.VMEM((...  1.71 us

profile of v5, /device:TPU:8, one launch (start us, length us, event | category | flops | bytes accessed | tf_op | source)
XLA Modules:
  0.0 73.3 jit_solution(12106631025454191065)
XLA Ops:
  1.3 1.7 %prepare.1 = (bf16[16,120,128]{2,1,0:T(8,128)(2,1)S(1)}, f32[2,256,128]{2,1,0:T(8,128)S(1)}) custom-call(f32[2]{0:T(128)} %w_hbm.1, s32[1]{0:T(128)S(6)} %copy.8.low_ref, s32[1]{0:T(128)S(6)} %copy.9.high_ref, bf16[2,256,256]{2,1,0:T(8,128)(2,1)} %p_ref.1, bf16[2,256,512]{2,1,0:T(8,128)(2,1)} %b_ref.1, bf16[32,256]{1,0:T(8,128)(2,1)} %l_ref.1, ...), custom_call_target="tpu_custom_call" | custom-call | tf_op jit(solution)/shard_map/prepare/pallas_call | solution.py:316
  3.0 27.4 %all_to_all.15 = bf16[16,120,128]{2,1,0:T(8,128)(2,1)S(1)} all-to-all(bf16[16,120,128]{2,1,0:T(8,128)(2,1)S(1)} %get-tuple-element.8), channel_id=1, replica_groups=mesh['energy'=16,'chip'=16,'core'=2] {'chip'}, dimensions={0} | all-to-all | bytes 983040 | tf_op jit(solution)/shard_map/all_to_all | solution.py:383
  30.5 2.5 %all-gather = bf16[32,120,128]{2,1,0:T(8,128)(2,1)S(1)} all-gather(bf16[16,120,128]{2,1,0:T(8,128)(2,1)S(1)} %all_to_all.15), channel_id=2, replica_groups=mesh['energy'=16,'chip'=16,'core'=2] {'core'}, dimensions={0}, use_global_device_ids=true | all-gather | bytes 1474560 | tf_op jit(solution)/shard_map/all_gather | solution.py:384
  33.0 0.0 copy-start.1
  33.0 0.0 copy-start.2
  33.0 0.0 copy-start.3
  33.0 5.0 %sweeps.1 = bf16[16,64,128]{2,1,0:T(8,128)(2,1)S(1)} custom-call(bf16[2,16,120,128]{3,2,1,0:T(8,128)(2,1)S(1)} %bitcast.3), custom_call_target="tpu_custom_call" | custom-call | tf_op jit(solution)/shard_map/sweeps/pallas_call | solution.py:336
  37.9 0.0 copy-start
  38.0 14.3 %all_to_all.16 = bf16[16,64,128]{2,1,0:T(8,128)(2,1)S(1)} all-to-all(bf16[16,64,128]{2,1,0:T(8,128)(2,1)S(1)} %sweeps.1), channel_id=1, replica_groups=mesh['energy'=16,'chip'=16,'core'=2] {'chip'}, dimensions={0} | all-to-all | bytes 524288 | tf_op jit(solution)/shard_map/all_to_all | solution.py:386
  52.3 0.0 copy-done.1
  52.3 0.0 copy-done.2
  52.3 0.0 copy-done.3
  52.3 0.0 copy-done
  52.3 1.1 %finish.1 = bf16[16,16,256]{2,1,0:T(8,128)(2,1)S(1)} custom-call(f32[2,256,128]{2,1,0:T(8,128)S(1)} %get-tuple-element.7.scale_ref, bf16[2,256,256]{2,1,0:T(8,128)(2,1)S(1)} %copy-done.1, bf16[2,256,512]{2,1,0:T(8,128)(2,1)S(1)} %copy-done, bf16[32,256]{1,0:T(8,128)(2,1)S(1)} %copy-done.2, bf16[32,256]{1,0:T(8,128)(2,1)S(1)} %copy-done.3, ...), custom_call_target="tpu_custom_call" | custom-call | tf_op jit(solution)/shard_map/finish/pallas_call | solution.py:353
  53.4 19.2 %all_to_all.17 = bf16[16,16,256]{2,1,0:T(8,128)(2,1)S(1)} all-to-all(bf16[16,16,256]{2,1,0:T(8,128)(2,1)S(1)} %finish.1), channel_id=1, replica_groups=mesh['energy'=16,'chip'=16,'core'=2] {'energy'}, dimensions={0} | all-to-all | bytes 262144 | tf_op jit(solution)/shard_map/all_to_all | solution.py:397
  72.7 0.6 convert_reduce_fusion
Async XLA Ops:
  33.0 19.3 %copy-start.1 = (bf16[2,256,256]{2,1,0:T(8,128)(2,1)S(1)}, bf16[2,256,256]{2,1,0:T(8,128)(2,1)}, u32[]{:S(2)}) copy-start(bf16[2,256,256]{2,1,0:T(8,128)(2,1)} %p_ref.1) | copy-start | bytes 786436
  33.0 19.3 %copy-start.2 = (bf16[32,256]{1,0:T(8,128)(2,1)S(1)}, bf16[32,256]{1,0:T(8,128)(2,1)}, u32[]{:S(2)}) copy-start(bf16[32,256]{1,0:T(8,128)(2,1)} %l_ref.1) | copy-start | bytes 49156
  33.0 19.3 %copy-start.3 = (bf16[32,256]{1,0:T(8,128)(2,1)S(1)}, bf16[32,256]{1,0:T(8,128)(2,1)}, u32[]{:S(2)}) copy-start(bf16[32,256]{1,0:T(8,128)(2,1)} %r_ref.1) | copy-start | bytes 49156
  37.9 14.4 %copy-start = (bf16[2,256,512]{2,1,0:T(8,128)(2,1)S(1)}, bf16[2,256,512]{2,1,0:T(8,128)(2,1)}, u32[]{:S(2)}) copy-start(bf16[2,256,512]{2,1,0:T(8,128)(2,1)} %b_ref.1) | copy-start | bytes 1572868

commit v6 on v5

--- a/solution.py
+++ b/solution.py
@@ -1,3 +1,5 @@
+import functools
+
 import jax
 import jax.numpy as jnp
 from jax import lax
@@ -17,6 +19,13 @@
 
 def mm_nt(a, b):
     return lax.dot_general(a, b, (((1,), (1,)), ((), ())), preferred_element_type=F32)
+
+
+SLOTS = 4
+
+
+def own_slot(chips):
+    return lax.axis_index("chip") // (chips // SLOTS)
 
 
 def pack(step, middle):
@@ -47,6 +56,7 @@
     p_ref,
     b_ref,
     c_ref,
+    q_ref,
     sems,
 ):
     count, block, modes = b_ref.shape
@@ -81,9 +91,15 @@
     weighted = [jnp.where(inside, u[e] * (2.0 * w_ref[e]), 0.0).astype(BF16) for e in energies]
     outer = [mm(weighted[e], p_ref[e]).astype(BF16) for e in energies]
     middle = [mm_nt(weighted[e], u[e].astype(BF16)) for e in energies]
+    slot = own_slot(o_ref.shape[0])
+    for e in energies:
+        blocks = [rim[e][:edge], rim[e][edge:], outer[e][:edge], outer[e][edge:]]
+        for i, rows in enumerate(blocks):
+            at = pl.multiple_of(((slot + i) & 3) * edge, edge)
+            q_ref[e, pl.ds(at, edge)] = rows
     fetch[4].wait()
     for e in energies:
-        rows = mm(jnp.concatenate([rim[e], outer[e]], axis=0), b_ref[e])
+        rows = mm(q_ref[e], b_ref[e])
         columns = rows.T.astype(BF16)
         exact = pack(step[e], middle[e])
         left = jnp.zeros_like(exact)
@@ -93,9 +109,6 @@
             left -= rounded.astype(F32)
             o_ref[e * each + k, chunk:] = rounded
             o_ref[e * each + k, :chunk] = columns[k * chunk : (k + 1) * chunk]
-
-
-SLOTS = 4
 
 
 def sweep_all(x_ref, o_ref, wf_ref, wa_ref, wk_ref):
@@ -154,36 +167,41 @@
         first, second = 1 if g == 0 else 0, -1 if g == last else 0
         plain = upper(g, 0)
         high = mm(upper(g, first) if first else plain, spread)
-        low = lower(g, second)
-        wf_ref[g, :LANES] = fit(high[:, :wide], first)
-        wf_ref[g, LANES:, :LANES] = fit(low[0], second)
+        low = lower(g, second - 1)
+        wf_ref[g, :LANES, :LANES] = fit(high[:, :LANES], first)
+        wf_ref[g, :LANES, LANES:] = fit(high[:, LANES:wide], first + 1)
+        wf_ref[g, LANES:, :LANES] = fit(low[0], second - 1)
         wf_ref[g, LANES:, LANES:] = fit(low[1], second)
-        wk_ref[g, :LANES] = fit(high[:, wide:], first)
-        wk_ref[g, LANES:, :LANES] = fit(mm_nt(spread_t, plain), second)
+        wk_ref[g, :LANES, :LANES] = fit(high[:, wide : 3 * LANES], first)
+        wk_ref[g, :LANES, LANES:] = fit(high[:, 3 * LANES :], first + 1)
+        wk_ref[g, LANES:, :LANES] = fit(mm_nt(spread_t, plain), second - 1)
         wk_ref[g, LANES:, LANES:] = fit(low[2], second)
         if first or second:
             if first:
                 high = mm(plain, spread)
             if second:
-                low = lower(g, 0)
+                low = lower(g, -1)
             at = 0 if first else 1
             wa_ref[at, :LANES, :LANES] = fit(high[:, :LANES], -second)
-            wa_ref[at, :LANES, LANES:] = fit(high[:, LANES:wide], -first)
-            wa_ref[at, LANES:, :LANES] = fit(low[0], -second)
+            wa_ref[at, :LANES, LANES:] = fit(high[:, LANES:wide], 1 - first)
+            wa_ref[at, LANES:, :LANES] = fit(low[0], -1 - second)
             wa_ref[at, LANES:, LANES:] = fit(low[1], -first)
 
-    at = lax.broadcasted_iota(jnp.int32, (1, 2 * wide), 1)
-    source = (((at >> 5) & 3) << 7) | ((at >> 7) << 5) | (at & 31)
-    order = lax.broadcasted_iota(jnp.int32, (2 * wide, 2 * wide), 0) == source
-    order = order.astype(F32).astype(BF16)
-    start = jnp.concatenate(
-        [
-            jnp.concatenate([strip(g + groups * j, slice(chunk)) for j in range(SLOTS)], axis=1)
-            for g in range(groups)
-        ],
-        axis=0,
-    )
-    start = mm(start, order)
+    lane = lane_slot[:, :LANES]
+
+    def choose(parts, shift):
+        got = parts[0]
+        for j in range(1, SLOTS):
+            got = jnp.where(lane == (j + shift) % SLOTS, parts[j], got)
+        return got
+
+    forward, adjoint = [], []
+    for g in range(groups):
+        parts = [strip(g + groups * j, slice(chunk)).astype(F32) for j in range(SLOTS)]
+        blocks = [choose(parts, i) for i in range(4)]
+        forward.append(jnp.concatenate(blocks[:2], axis=1))
+        halves = [pltpu.roll(v, 2 * edge, 1) for v in blocks[2:]]
+        adjoint.append(jnp.concatenate(halves, axis=1))
 
     def up(parts, at):
         return [parts[-1]] + parts[:-1] if at == 1 else list(parts)
@@ -239,33 +257,30 @@
             got[g] = gets_behind[i]
         return got
 
-    base = [start[g * chunk : (g + 1) * chunk, :wide] for g in range(groups)]
-    z = iterate(base, lambda v, g: mm(v, wf_ref[g]), True)
-    base = [
-        start[g * chunk : (g + 1) * chunk, wide:] + mm(z[g], wk_ref[g]) for g in range(groups)
-    ]
+    z = iterate(forward, lambda v, g: mm(v, wf_ref[g]), True)
+    base = [adjoint[g] + mm(z[g], wk_ref[g]) for g in range(groups)]
     ends = {0: wa_ref.at[0], last: wa_ref.at[1]}
     y = iterate(base, lambda v, g: mm_nt(v, ends[g][...] if g in ends else wf_ref[g]), False)
-    out = [jnp.concatenate(v, axis=1) for v in zip(turned(z, True), turned(y, False))]
-    out = [jnp.where(core == 0, out[g], out[g + 1]) for g in evens]
-    out = mm(jnp.concatenate(out, axis=0), order).astype(BF16)
+    z, y = turned(z, True), turned(y, False)
     for i, g in enumerate(evens):
+        own = [jnp.where(core == 0, v[g], v[g + 1]).astype(F32) for v in (y, z)]
+        parts = [own[0][:, :LANES], own[0][:, LANES:]]
+        parts += [pltpu.roll(own[1][:, v], 2 * edge, 1) for v in (slice(LANES), slice(LANES, wide))]
         for j in range(SLOTS):
-            o_ref[(g + groups * j) // 2] = out[
-                i * chunk : (i + 1) * chunk, j * LANES : (j + 1) * LANES
-            ]
-
-
-def finish(scale_ref, p_ref, b_ref, l_ref, r_ref, zy_ref, o_ref):
+            o_ref[(g + groups * j) // 2] = choose(parts, j).astype(BF16)
+
+
+def finish(chips, scale_ref, p_ref, b_ref, l_ref, r_ref, zy_ref, o_ref):
     count, block, modes = b_ref.shape
     edge = l_ref.shape[0]
-    couple = jnp.concatenate([l_ref[...], r_ref[...]], axis=0).astype(F32).T.astype(BF16)
-    couple = jnp.concatenate([couple, jnp.zeros_like(couple)], axis=1)
+    couple = jnp.concatenate([l_ref[...], r_ref[...]], axis=0).astype(F32).T
     pick = (
-        lax.broadcasted_iota(jnp.int32, (2 * edge, LANES), 0) + 2 * edge
+        lax.broadcasted_iota(jnp.int32, (2 * edge, LANES), 0)
         == lax.broadcasted_iota(jnp.int32, (2 * edge, LANES), 1)
-    ).astype(F32).astype(BF16)
-    front = jnp.concatenate([couple, pick], axis=0)
+    ).astype(F32)
+    front = jnp.concatenate([jnp.zeros_like(couple), couple], axis=1)
+    front = jnp.concatenate([front, pick], axis=0)
+    front = pltpu.roll(front, own_slot(chips) * edge, 1).astype(BF16)
     energies = range(count)
     got = [mm_nt(front, zy_ref[e]) for e in energies]
     rhs = [(b_ref[e].astype(F32) + got[e][:block]).astype(BF16) for e in energies]
@@ -323,6 +338,7 @@
             pltpu.VMEM((count, block, block), BF16),
             pltpu.VMEM((count, block, modes), BF16),
             pltpu.VMEM((2 * edge, block), BF16),
+            pltpu.VMEM((count, 4 * edge, block), BF16),
             pltpu.SemaphoreType.DMA((5,)),
         ],
         name="prepare",
@@ -348,10 +364,10 @@
     )(given)
 
 
-def call_finish(scale, inverse, source, left, right, columns, energies, owned):
+def call_finish(scale, inverse, source, left, right, columns, energies, owned, chips):
     block = inverse.shape[1]
     return pl.pallas_call(
-        finish,
+        functools.partial(finish, chips),
         out_shape=shape((energies, owned, block), BF16),
         in_specs=[VMEM] * 6,
         out_specs=VMEM,
@@ -393,6 +409,7 @@
         out.reshape(count, modes, 4 * edge),
         energies,
         owned,
+        chips,
     )
     out = lax.all_to_all(out, "energy", 0, 0, tiled=True)
     return jnp.sum(out.astype(F32), axis=0)[None]

time: 73.6 us -> 73.2 us (level)
  no operation moved by 1% of the time
where the time goes in v6:
time: 73.2 us; the launch traced here: 72.9 us
  blocking collectives  63.5 us (87%)
  Pallas kernels  7.44 us (10%)
  between operations  1.34 us (2%)
    all_to_all x1, blocking collectives, body(): mine = lax.all_to_all(pieces, 'chip', 0, 0, tiled=True)  27.4 us
    all_to_all x1, blocking collectives, body(): out = lax.all_to_all(out, 'energy', 0, 0, tiled=True)  19.2 us
    all_to_all x1, blocking collectives, body(): out = lax.all_to_all(out, 'chip', 0, 0, tiled=True)  14.3 us
    pallas_call x1, Pallas kernels, call_sweeps(): pl.pallas_call(sweep_all, out_shape=shape((chips, chunk, lanes), BF16), i...  4.37 us
    all_gather x1, blocking collectives, body(): given = lax.all_gather(mine, 'core')  2.5 us
    pallas_call x1, Pallas kernels, call_prepare(): pl.pallas_call(prepare, out_shape=(pltpu.VMEM(pieces, BF16), pltpu.VMEM((...  1.71 us

profile of v6, /device:TPU:8, one launch (start us, length us, event | category | flops | bytes accessed | tf_op | source)
XLA Modules:
  0.0 72.9 jit_solution(5609339907612523503)
XLA Ops:
  1.3 1.7 %prepare.1 = (bf16[16,120,128]{2,1,0:T(8,128)(2,1)S(1)}, f32[2,256,128]{2,1,0:T(8,128)S(1)}) custom-call(f32[2]{0:T(128)} %w_hbm.1, s32[1]{0:T(128)S(6)} %copy.8.low_ref, s32[1]{0:T(128)S(6)} %copy.9.high_ref, bf16[2,256,256]{2,1,0:T(8,128)(2,1)} %p_ref.1, bf16[2,256,512]{2,1,0:T(8,128)(2,1)} %b_ref.1, bf16[32,256]{1,0:T(8,128)(2,1)} %l_ref.1, ...), custom_call_target="tpu_custom_call" | custom-call | tf_op jit(solution)/shard_map/prepare/pallas_call | solution.py:331
  3.0 27.4 %all_to_all.15 = bf16[16,120,128]{2,1,0:T(8,128)(2,1)S(1)} all-to-all(bf16[16,120,128]{2,1,0:T(8,128)(2,1)S(1)} %get-tuple-element.8), channel_id=1, replica_groups=mesh['energy'=16,'chip'=16,'core'=2] {'chip'}, dimensions={0} | all-to-all | bytes 983040 | tf_op jit(solution)/shard_map/all_to_all | solution.py:399
  30.5 2.5 %all-gather = bf16[32,120,128]{2,1,0:T(8,128)(2,1)S(1)} all-gather(bf16[16,120,128]{2,1,0:T(8,128)(2,1)S(1)} %all_to_all.15), channel_id=2, replica_groups=mesh['energy'=16,'chip'=16,'core'=2] {'core'}, dimensions={0}, use_global_device_ids=true | all-gather | bytes 1474560 | tf_op jit(solution)/shard_map/all_gather | solution.py:400
  33.0 0.0 copy-start.1
  33.0 0.0 copy-start.2
  33.0 0.0 copy-start.3
  33.0 4.4 %sweeps.1 = bf16[16,64,128]{2,1,0:T(8,128)(2,1)S(1)} custom-call(bf16[2,16,120,128]{3,2,1,0:T(8,128)(2,1)S(1)} %bitcast.3), custom_call_target="tpu_custom_call" | custom-call | tf_op jit(solution)/shard_map/sweeps/pallas_call | solution.py:352
  37.3 0.0 copy-start
  37.4 14.3 %all_to_all.16 = bf16[16,64,128]{2,1,0:T(8,128)(2,1)S(1)} all-to-all(bf16[16,64,128]{2,1,0:T(8,128)(2,1)S(1)} %sweeps.1), channel_id=1, replica_groups=mesh['energy'=16,'chip'=16,'core'=2] {'chip'}, dimensions={0} | all-to-all | bytes 524288 | tf_op jit(solution)/shard_map/all_to_all | solution.py:402
  51.7 0.0 copy-done.1
  51.7 0.0 copy-done.2
  51.7 0.0 copy-done.3
  51.7 0.0 copy-done
  51.7 1.4 %finish.1 = bf16[16,16,256]{2,1,0:T(8,128)(2,1)S(1)} custom-call(f32[2,256,128]{2,1,0:T(8,128)S(1)} %get-tuple-element.7.scale_ref, bf16[2,256,256]{2,1,0:T(8,128)(2,1)S(1)} %copy-done.1, bf16[2,256,512]{2,1,0:T(8,128)(2,1)S(1)} %copy-done, bf16[32,256]{1,0:T(8,128)(2,1)S(1)} %copy-done.2, bf16[32,256]{1,0:T(8,128)(2,1)S(1)} %copy-done.3, ...), custom_call_target="tpu_custom_call" | custom-call | tf_op jit(solution)/shard_map/finish/pallas_call | solution.py:369
  53.1 19.2 %all_to_all.17 = bf16[16,16,256]{2,1,0:T(8,128)(2,1)S(1)} all-to-all(bf16[16,16,256]{2,1,0:T(8,128)(2,1)S(1)} %finish.1), channel_id=1, replica_groups=mesh['energy'=16,'chip'=16,'core'=2] {'energy'}, dimensions={0} | all-to-all | bytes 262144 | tf_op jit(solution)/shard_map/all_to_all | solution.py:414
  72.3 0.6 convert_reduce_fusion
Async XLA Ops:
  33.0 18.7 %copy-start.1 = (bf16[2,256,256]{2,1,0:T(8,128)(2,1)S(1)}, bf16[2,256,256]{2,1,0:T(8,128)(2,1)}, u32[]{:S(2)}) copy-start(bf16[2,256,256]{2,1,0:T(8,128)(2,1)} %p_ref.1) | copy-start | bytes 786436
  33.0 18.7 %copy-start.2 = (bf16[32,256]{1,0:T(8,128)(2,1)S(1)}, bf16[32,256]{1,0:T(8,128)(2,1)}, u32[]{:S(2)}) copy-start(bf16[32,256]{1,0:T(8,128)(2,1)} %l_ref.1) | copy-start | bytes 49156
  33.0 18.7 %copy-start.3 = (bf16[32,256]{1,0:T(8,128)(2,1)S(1)}, bf16[32,256]{1,0:T(8,128)(2,1)}, u32[]{:S(2)}) copy-start(bf16[32,256]{1,0:T(8,128)(2,1)} %r_ref.1) | copy-start | bytes 49156
  37.3 14.4 %copy-start = (bf16[2,256,512]{2,1,0:T(8,128)(2,1)S(1)}, bf16[2,256,512]{2,1,0:T(8,128)(2,1)}, u32[]{:S(2)}) copy-start(bf16[2,256,512]{2,1,0:T(8,128)(2,1)} %b_ref.1) | copy-start | bytes 1572868

commit v7 on v6

--- a/solution.py
+++ b/solution.py
@@ -197,8 +197,8 @@
 
     forward, adjoint = [], []
     for g in range(groups):
-        parts = [strip(g + groups * j, slice(chunk)).astype(F32) for j in range(SLOTS)]
-        blocks = [choose(parts, i) for i in range(4)]
+        parts = [strip(g + groups * j, slice(chunk)) for j in range(SLOTS)]
+        blocks = [choose(parts, i).astype(F32) for i in range(4)]
         forward.append(jnp.concatenate(blocks[:2], axis=1))
         halves = [pltpu.roll(v, 2 * edge, 1) for v in blocks[2:]]
         adjoint.append(jnp.concatenate(halves, axis=1))
@@ -270,29 +270,34 @@
             o_ref[(g + groups * j) // 2] = choose(parts, j).astype(BF16)
 
 
-def finish(chips, scale_ref, p_ref, b_ref, l_ref, r_ref, zy_ref, o_ref):
+def finish(chips, scale_ref, p_ref, b_ref, l_ref, r_ref, zy_ref, o_ref, front_ref):
     count, block, modes = b_ref.shape
     edge = l_ref.shape[0]
-    couple = jnp.concatenate([l_ref[...], r_ref[...]], axis=0).astype(F32).T
-    pick = (
-        lax.broadcasted_iota(jnp.int32, (2 * edge, LANES), 0)
-        == lax.broadcasted_iota(jnp.int32, (2 * edge, LANES), 1)
-    ).astype(F32)
-    front = jnp.concatenate([jnp.zeros_like(couple), couple], axis=1)
-    front = jnp.concatenate([front, pick], axis=0)
-    front = pltpu.roll(front, own_slot(chips) * edge, 1).astype(BF16)
+    slot = own_slot(chips)
+    row = lax.broadcasted_iota(jnp.int32, (edge, LANES), 0)
+    column = lax.broadcasted_iota(jnp.int32, (edge, LANES), 1)
+    zero = jnp.zeros((edge, block), F32)
+    rows = [
+        jnp.concatenate([(column == row + i * edge).astype(F32), right], axis=1)
+        for i, right in enumerate([zero, zero, l_ref[...].astype(F32), r_ref[...].astype(F32)])
+    ]
+    for i, value in enumerate(rows):
+        if i > 1:
+            value = jnp.where(lax.broadcasted_iota(jnp.int32, value.shape, 1) < LANES, 0.0, value)
+        front_ref[pl.ds(pl.multiple_of(((slot + i) & 3) * edge, edge), edge)] = value
+    front = front_ref[...].T.astype(BF16)
     energies = range(count)
     got = [mm_nt(front, zy_ref[e]) for e in energies]
-    rhs = [(b_ref[e].astype(F32) + got[e][:block]).astype(BF16) for e in energies]
+    rhs = [(b_ref[e].astype(F32) + got[e][LANES:]).astype(BF16) for e in energies]
     psi = [mm(p_ref[e], rhs[e]).astype(BF16) for e in energies]
     scale = [jnp.concatenate([scale_ref[e]] * (modes // LANES), axis=1) for e in energies]
     source = [psi[e].astype(F32) * scale[e] for e in energies]
     update = [
         jnp.concatenate(
             [
-                source[e][:edge] + got[e][block + edge :],
+                source[e][:edge] + got[e][edge : 2 * edge],
                 source[e][edge : block - edge],
-                source[e][block - edge :] + got[e][block : block + edge],
+                source[e][block - edge :] + got[e][:edge],
             ],
             axis=0,
         ).astype(BF16)
@@ -371,6 +376,7 @@
         out_shape=shape((energies, owned, block), BF16),
         in_specs=[VMEM] * 6,
         out_specs=VMEM,
+        scratch_shapes=[pltpu.VMEM((LANES, LANES + block), F32)],
         name="finish",
         **PARAMS,
     )(scale, inverse, source, left, right, columns)

time: 73.2 us -> 72.9 us (level)
  no operation moved by 1% of the time
where the time goes in v7:
time: 72.9 us; the launch traced here: 72.6 us
  blocking collectives  63.5 us (87%)
  Pallas kernels  7.16 us (10%)
  between operations  1.34 us (2%)
    all_to_all x1, blocking collectives, body(): mine = lax.all_to_all(pieces, 'chip', 0, 0, tiled=True)  27.4 us
    all_to_all x1, blocking collectives, body(): out = lax.all_to_all(out, 'energy', 0, 0, tiled=True)  19.2 us
    all_to_all x1, blocking collectives, body(): out = lax.all_to_all(out, 'chip', 0, 0, tiled=True)  14.3 us
    pallas_call x1, Pallas kernels, call_sweeps(): pl.pallas_call(sweep_all, out_shape=shape((chips, chunk, lanes), BF16), i...  4.24 us
    all_gather x1, blocking collectives, body(): given = lax.all_gather(mine, 'core')  2.5 us
    pallas_call x1, Pallas kernels, call_prepare(): pl.pallas_call(prepare, out_shape=(pltpu.VMEM(pieces, BF16), pltpu.VMEM((...  1.71 us

profile of v7, /device:TPU:8, one launch (start us, length us, event | category | flops | bytes accessed | tf_op | source)
XLA Modules:
  0.0 72.6 jit_solution(6528398201359355712)
XLA Ops:
  1.3 1.7 %prepare.1 = (bf16[16,120,128]{2,1,0:T(8,128)(2,1)S(1)}, f32[2,256,128]{2,1,0:T(8,128)S(1)}) custom-call(f32[2]{0:T(128)} %w_hbm.1, s32[1]{0:T(128)S(6)} %copy.8.low_ref, s32[1]{0:T(128)S(6)} %copy.9.high_ref, bf16[2,256,256]{2,1,0:T(8,128)(2,1)} %p_ref.1, bf16[2,256,512]{2,1,0:T(8,128)(2,1)} %b_ref.1, bf16[32,256]{1,0:T(8,128)(2,1)} %l_ref.1, ...), custom_call_target="tpu_custom_call" | custom-call | tf_op jit(solution)/shard_map/prepare/pallas_call | solution.py:336
  3.0 27.4 %all_to_all.15 = bf16[16,120,128]{2,1,0:T(8,128)(2,1)S(1)} all-to-all(bf16[16,120,128]{2,1,0:T(8,128)(2,1)S(1)} %get-tuple-element.8), channel_id=1, replica_groups=mesh['energy'=16,'chip'=16,'core'=2] {'chip'}, dimensions={0} | all-to-all | bytes 983040 | tf_op jit(solution)/shard_map/all_to_all | solution.py:405
  30.5 2.5 %all-gather = bf16[32,120,128]{2,1,0:T(8,128)(2,1)S(1)} all-gather(bf16[16,120,128]{2,1,0:T(8,128)(2,1)S(1)} %all_to_all.15), channel_id=2, replica_groups=mesh['energy'=16,'chip'=16,'core'=2] {'core'}, dimensions={0}, use_global_device_ids=true | all-gather | bytes 1474560 | tf_op jit(solution)/shard_map/all_gather | solution.py:406
  33.0 0.0 copy-start.1
  33.0 0.0 copy-start.2
  33.0 0.0 copy-start.3
  33.0 4.2 %sweeps.1 = bf16[16,64,128]{2,1,0:T(8,128)(2,1)S(1)} custom-call(bf16[2,16,120,128]{3,2,1,0:T(8,128)(2,1)S(1)} %bitcast.3), custom_call_target="tpu_custom_call" | custom-call | tf_op jit(solution)/shard_map/sweeps/pallas_call | solution.py:357
  37.2 0.0 copy-start
  37.2 14.3 %all_to_all.16 = bf16[16,64,128]{2,1,0:T(8,128)(2,1)S(1)} all-to-all(bf16[16,64,128]{2,1,0:T(8,128)(2,1)S(1)} %sweeps.1), channel_id=1, replica_groups=mesh['energy'=16,'chip'=16,'core'=2] {'chip'}, dimensions={0} | all-to-all | bytes 524288 | tf_op jit(solution)/shard_map/all_to_all | solution.py:408
  51.6 0.0 copy-done.1
  51.6 0.0 copy-done.2
  51.6 0.0 copy-done.3
  51.6 0.0 copy-done
  51.6 1.2 %finish.1 = bf16[16,16,256]{2,1,0:T(8,128)(2,1)S(1)} custom-call(f32[2,256,128]{2,1,0:T(8,128)S(1)} %get-tuple-element.7.scale_ref, bf16[2,256,256]{2,1,0:T(8,128)(2,1)S(1)} %copy-done.1, bf16[2,256,512]{2,1,0:T(8,128)(2,1)S(1)} %copy-done, bf16[32,256]{1,0:T(8,128)(2,1)S(1)} %copy-done.2, bf16[32,256]{1,0:T(8,128)(2,1)S(1)} %copy-done.3, ...), custom_call_target="tpu_custom_call" | custom-call | tf_op jit(solution)/shard_map/finish/pallas_call | solution.py:374
  52.8 19.2 %all_to_all.17 = bf16[16,16,256]{2,1,0:T(8,128)(2,1)S(1)} all-to-all(bf16[16,16,256]{2,1,0:T(8,128)(2,1)S(1)} %finish.1), channel_id=1, replica_groups=mesh['energy'=16,'chip'=16,'core'=2] {'energy'}, dimensions={0} | all-to-all | bytes 262144 | tf_op jit(solution)/shard_map/all_to_all | solution.py:420
  72.0 0.6 convert_reduce_fusion
Async XLA Ops:
  33.0 18.6 %copy-start.1 = (bf16[2,256,256]{2,1,0:T(8,128)(2,1)S(1)}, bf16[2,256,256]{2,1,0:T(8,128)(2,1)}, u32[]{:S(2)}) copy-start(bf16[2,256,256]{2,1,0:T(8,128)(2,1)} %p_ref.1) | copy-start | bytes 786436
  33.0 18.6 %copy-start.2 = (bf16[32,256]{1,0:T(8,128)(2,1)S(1)}, bf16[32,256]{1,0:T(8,128)(2,1)}, u32[]{:S(2)}) copy-start(bf16[32,256]{1,0:T(8,128)(2,1)} %l_ref.1) | copy-start | bytes 49156
  33.0 18.6 %copy-start.3 = (bf16[32,256]{1,0:T(8,128)(2,1)S(1)}, bf16[32,256]{1,0:T(8,128)(2,1)}, u32[]{:S(2)}) copy-start(bf16[32,256]{1,0:T(8,128)(2,1)} %r_ref.1) | copy-start | bytes 49156
  37.2 14.4 %copy-start = (bf16[2,256,512]{2,1,0:T(8,128)(2,1)S(1)}, bf16[2,256,512]{2,1,0:T(8,128)(2,1)}, u32[]{:S(2)}) copy-start(bf16[2,256,512]{2,1,0:T(8,128)(2,1)} %b_ref.1) | copy-start | bytes 1572868

commit v8 on v7

--- a/solution.py
+++ b/solution.py
@@ -52,11 +52,13 @@
     r_hbm,
     o_ref,
     scale_ref,
+    front_ref,
     w_ref,
     p_ref,
     b_ref,
     c_ref,
     q_ref,
+    f_ref,
     sems,
 ):
     count, block, modes = b_ref.shape
@@ -79,8 +81,22 @@
         scale_ref[e] = jnp.where(inside, 2.0 * w_ref[e], 0.0)
     at = lax.broadcasted_iota(jnp.int32, (1, block), 1)
     inside = (at >= low) & (at < high)
-    for copy in fetch[1:4]:
-        copy.wait()
+    fetch[1].wait()
+    fetch[2].wait()
+    slot = own_slot(o_ref.shape[0])
+    row = lax.broadcasted_iota(jnp.int32, (edge, LANES), 0)
+    column = lax.broadcasted_iota(jnp.int32, (edge, LANES), 1)
+    zero = jnp.zeros((edge, block), F32)
+    rows = [
+        jnp.concatenate([(column == row + i * edge).astype(F32), right], axis=1)
+        for i, right in enumerate([zero, zero, c_ref[:edge].astype(F32), c_ref[edge:].astype(F32)])
+    ]
+    for i, value in enumerate(rows):
+        if i > 1:
+            value = jnp.where(lax.broadcasted_iota(jnp.int32, value.shape, 1) < LANES, 0.0, value)
+        f_ref[pl.ds(pl.multiple_of(((slot + i) & 3) * edge, edge), edge)] = value
+    front_ref[...] = f_ref[...].T.astype(BF16)
+    fetch[3].wait()
     couple = c_ref[...]
     each = o_ref.shape[0] // count
     chunk = modes // each
@@ -91,7 +107,6 @@
     weighted = [jnp.where(inside, u[e] * (2.0 * w_ref[e]), 0.0).astype(BF16) for e in energies]
     outer = [mm(weighted[e], p_ref[e]).astype(BF16) for e in energies]
     middle = [mm_nt(weighted[e], u[e].astype(BF16)) for e in energies]
-    slot = own_slot(o_ref.shape[0])
     for e in energies:
         blocks = [rim[e][:edge], rim[e][edge:], outer[e][:edge], outer[e][edge:]]
         for i, rows in enumerate(blocks):
@@ -270,24 +285,10 @@
             o_ref[(g + groups * j) // 2] = choose(parts, j).astype(BF16)
 
 
-def finish(chips, scale_ref, p_ref, b_ref, l_ref, r_ref, zy_ref, o_ref, front_ref):
+def finish(edge, scale_ref, front_ref, p_ref, b_ref, zy_ref, o_ref):
     count, block, modes = b_ref.shape
-    edge = l_ref.shape[0]
-    slot = own_slot(chips)
-    row = lax.broadcasted_iota(jnp.int32, (edge, LANES), 0)
-    column = lax.broadcasted_iota(jnp.int32, (edge, LANES), 1)
-    zero = jnp.zeros((edge, block), F32)
-    rows = [
-        jnp.concatenate([(column == row + i * edge).astype(F32), right], axis=1)
-        for i, right in enumerate([zero, zero, l_ref[...].astype(F32), r_ref[...].astype(F32)])
-    ]
-    for i, value in enumerate(rows):
-        if i > 1:
-            value = jnp.where(lax.broadcasted_iota(jnp.int32, value.shape, 1) < LANES, 0.0, value)
-        front_ref[pl.ds(pl.multiple_of(((slot + i) & 3) * edge, edge), edge)] = value
-    front = front_ref[...].T.astype(BF16)
     energies = range(count)
-    got = [mm_nt(front, zy_ref[e]) for e in energies]
+    got = [mm_nt(front_ref[...], zy_ref[e]) for e in energies]
     rhs = [(b_ref[e].astype(F32) + got[e][LANES:]).astype(BF16) for e in energies]
     psi = [mm(p_ref[e], rhs[e]).astype(BF16) for e in energies]
     scale = [jnp.concatenate([scale_ref[e]] * (modes // LANES), axis=1) for e in energies]
@@ -335,15 +336,20 @@
     pieces = (chips, count * modes // chips + edge + edge * 3 // 4, 4 * edge)
     return pl.pallas_call(
         prepare,
-        out_shape=(pltpu.VMEM(pieces, BF16), pltpu.VMEM((count, block, LANES), F32)),
+        out_shape=(
+            pltpu.VMEM(pieces, BF16),
+            pltpu.VMEM((count, block, LANES), F32),
+            pltpu.VMEM((LANES + block, LANES), BF16),
+        ),
         in_specs=[ANY, SMEM, SMEM] + [ANY] * 4,
-        out_specs=(VMEM, VMEM),
+        out_specs=(VMEM, VMEM, VMEM),
         scratch_shapes=[
             pltpu.SMEM((count,), F32),
             pltpu.VMEM((count, block, block), BF16),
             pltpu.VMEM((count, block, modes), BF16),
             pltpu.VMEM((2 * edge, block), BF16),
             pltpu.VMEM((count, 4 * edge, block), BF16),
+            pltpu.VMEM((LANES, LANES + block), F32),
             pltpu.SemaphoreType.DMA((5,)),
         ],
         name="prepare",
@@ -369,17 +375,16 @@
     )(given)
 
 
-def call_finish(scale, inverse, source, left, right, columns, energies, owned, chips):
+def call_finish(scale, front, inverse, source, columns, energies, owned):
     block = inverse.shape[1]
     return pl.pallas_call(
-        functools.partial(finish, chips),
+        functools.partial(finish, columns.shape[2] // 4),
         out_shape=shape((energies, owned, block), BF16),
-        in_specs=[VMEM] * 6,
+        in_specs=[VMEM] * 5,
         out_specs=VMEM,
-        scratch_shapes=[pltpu.VMEM((LANES, LANES + block), F32)],
         name="finish",
         **PARAMS,
-    )(scale, inverse, source, left, right, columns)
+    )(scale, front, inverse, source, columns)
 
 
 def body(
@@ -399,7 +404,7 @@
     owned = block // energies
     scalars = (energy_weights, collector_low, collector_high)
 
-    pieces, scale = call_prepare(
+    pieces, scale, front = call_prepare(
         scalars, inverse_blocks, source, left_coupling, right_coupling, chips
     )
     mine = lax.all_to_all(pieces, "chip", 0, 0, tiled=True)
@@ -408,14 +413,12 @@
     out = lax.all_to_all(out, "chip", 0, 0, tiled=True)
     out = call_finish(
         scale,
+        front,
         inverse_blocks,
         source,
-        left_coupling,
-        right_coupling,
         out.reshape(count, modes, 4 * edge),
         energies,
         owned,
-        chips,
     )
     out = lax.all_to_all(out, "energy", 0, 0, tiled=True)
     return jnp.sum(out.astype(F32), axis=0)[None]

time: 72.9 us -> 72.8 us (level)
  no operation moved by 1% of the time
where the time goes in v8:
time: 72.8 us; the launch traced here: 72.5 us
  blocking collectives  63.5 us (87%)
  Pallas kernels  7.07 us (10%)
  between operations  1.33 us (2%)
    all_to_all x1, blocking collectives, body(): mine = lax.all_to_all(pieces, 'chip', 0, 0, tiled=True)  27.4 us
    all_to_all x1, blocking collectives, body(): out = lax.all_to_all(out, 'energy', 0, 0, tiled=True)  19.2 us
    all_to_all x1, blocking collectives, body(): out = lax.all_to_all(out, 'chip', 0, 0, tiled=True)  14.3 us
    pallas_call x1, Pallas kernels, call_sweeps(): pl.pallas_call(sweep_all, out_shape=shape((chips, chunk, lanes), BF16), i...  4.23 us
    all_gather x1, blocking collectives, body(): given = lax.all_gather(mine, 'core')  2.5 us
    pallas_call x1, Pallas kernels, call_prepare(): pl.pallas_call(prepare, out_shape=(pltpu.VMEM(pieces, BF16), pltpu.VMEM((...  1.71 us

profile of v8, /device:TPU:8, one launch (start us, length us, event | category | flops | bytes accessed | tf_op | source)
XLA Modules:
  0.0 72.5 jit_solution(7572464739118776047)
XLA Ops:
  1.3 1.7 %prepare.1 = (bf16[16,120,128]{2,1,0:T(8,128)(2,1)S(1)}, f32[2,256,128]{2,1,0:T(8,128)S(1)}, bf16[384,128]{1,0:T(8,128)(2,1)S(1)}) custom-call(f32[2]{0:T(128)} %w_hbm.1, s32[1]{0:T(128)S(6)} %copy.8.low_ref, s32[1]{0:T(128)S(6)} %copy.9.high_ref, bf16[2,256,256]{2,1,0:T(8,128)(2,1)} %p_ref.1, bf16[2,256,512]{2,1,0:T(8,128)(2,1)} %b_ref.1, ...), custom_call_target="tpu_custom_call" | custom-call | tf_op jit(solution)/shard_map/prepare/pallas_call | solution.py:337
  3.0 27.4 %all_to_all.15 = bf16[16,120,128]{2,1,0:T(8,128)(2,1)S(1)} all-to-all(bf16[16,120,128]{2,1,0:T(8,128)(2,1)S(1)} %get-tuple-element.10), channel_id=1, replica_groups=mesh['energy'=16,'chip'=16,'core'=2] {'chip'}, dimensions={0} | all-to-all | bytes 983040 | tf_op jit(solution)/shard_map/all_to_all | solution.py:410
  30.5 2.5 %all-gather = bf16[32,120,128]{2,1,0:T(8,128)(2,1)S(1)} all-gather(bf16[16,120,128]{2,1,0:T(8,128)(2,1)S(1)} %all_to_all.15), channel_id=2, replica_groups=mesh['energy'=16,'chip'=16,'core'=2] {'core'}, dimensions={0}, use_global_device_ids=true | all-gather | bytes 1474560 | tf_op jit(solution)/shard_map/all_gather | solution.py:411
  33.0 0.0 copy-start.1
  33.0 4.2 %sweeps.1 = bf16[16,64,128]{2,1,0:T(8,128)(2,1)S(1)} custom-call(bf16[2,16,120,128]{3,2,1,0:T(8,128)(2,1)S(1)} %bitcast.3), custom_call_target="tpu_custom_call" | custom-call | tf_op jit(solution)/shard_map/sweeps/pallas_call | solution.py:363
  37.2 0.0 copy-start
  37.2 14.3 %all_to_all.16 = bf16[16,64,128]{2,1,0:T(8,128)(2,1)S(1)} all-to-all(bf16[16,64,128]{2,1,0:T(8,128)(2,1)S(1)} %sweeps.1), channel_id=1, replica_groups=mesh['energy'=16,'chip'=16,'core'=2] {'chip'}, dimensions={0} | all-to-all | bytes 524288 | tf_op jit(solution)/shard_map/all_to_all | solution.py:413
  51.5 0.0 copy-done.1
  51.6 0.0 copy-done
  51.6 1.1 %finish.1 = bf16[16,16,256]{2,1,0:T(8,128)(2,1)S(1)} custom-call(f32[2,256,128]{2,1,0:T(8,128)S(1)} %get-tuple-element.8.scale_ref, bf16[384,128]{1,0:T(8,128)(2,1)S(1)} %get-tuple-element.9.front_ref, bf16[2,256,256]{2,1,0:T(8,128)(2,1)S(1)} %copy-done.1, bf16[2,256,512]{2,1,0:T(8,128)(2,1)S(1)} %copy-done, bf16[2,512,128]{2,1,0:T(8,128)(2,1)S(1)} %bitcast.4), custom_call_target="tpu_custom_call" | custom-call | tf_op jit(solution)/shard_map/finish/pallas_call | solution.py:380
  52.7 19.2 %all_to_all.17 = bf16[16,16,256]{2,1,0:T(8,128)(2,1)S(1)} all-to-all(bf16[16,16,256]{2,1,0:T(8,128)(2,1)S(1)} %finish.1), channel_id=1, replica_groups=mesh['energy'=16,'chip'=16,'core'=2] {'energy'}, dimensions={0} | all-to-all | bytes 262144 | tf_op jit(solution)/shard_map/all_to_all | solution.py:423
  71.9 0.6 convert_reduce_fusion
Async XLA Ops:
  33.0 18.6 %copy-start.1 = (bf16[2,256,256]{2,1,0:T(8,128)(2,1)S(1)}, bf16[2,256,256]{2,1,0:T(8,128)(2,1)}, u32[]{:S(2)}) copy-start(bf16[2,256,256]{2,1,0:T(8,128)(2,1)} %p_ref.1) | copy-start | bytes 786436
  37.2 14.4 %copy-start = (bf16[2,256,512]{2,1,0:T(8,128)(2,1)S(1)}, bf16[2,256,512]{2,1,0:T(8,128)(2,1)}, u32[]{:S(2)}) copy-start(bf16[2,256,512]{2,1,0:T(8,128)(2,1)} %b_ref.1) | copy-start | bytes 1572868

commit v9 on v8

--- a/solution.py
+++ b/solution.py
@@ -71,8 +71,8 @@
         (b_hbm, b_ref),
     ]
     fetch = [pltpu.make_async_copy(*ends, sems.at[i]) for i, ends in enumerate(fetch)]
-    for copy in fetch:
-        copy.start()
+    for i in (3, 1, 2, 0, 4):
+        fetch[i].start()
     fetch[0].wait()
     low, high = low_ref[0], high_ref[0]
     at = lax.broadcasted_iota(jnp.int32, (block, LANES), 0)

time: 72.8 us -> 72.8 us (level)
  no operation moved by 1% of the time
where the time goes in v9:
time: 72.8 us; the launch traced here: 72.5 us
  blocking collectives  63.5 us (87%)
  Pallas kernels  7.07 us (10%)
  between operations  1.33 us (2%)
    all_to_all x1, blocking collectives, body(): mine = lax.all_to_all(pieces, 'chip', 0, 0, tiled=True)  27.4 us
    all_to_all x1, blocking collectives, body(): out = lax.all_to_all(out, 'energy', 0, 0, tiled=True)  19.2 us
    all_to_all x1, blocking collectives, body(): out = lax.all_to_all(out, 'chip', 0, 0, tiled=True)  14.3 us
    pallas_call x1, Pallas kernels, call_sweeps(): pl.pallas_call(sweep_all, out_shape=shape((chips, chunk, lanes), BF16), i...  4.23 us
    all_gather x1, blocking collectives, body(): given = lax.all_gather(mine, 'core')  2.5 us
    pallas_call x1, Pallas kernels, call_prepare(): pl.pallas_call(prepare, out_shape=(pltpu.VMEM(pieces, BF16), pltpu.VMEM((...  1.71 us

profile of v9, /device:TPU:8, one launch (start us, length us, event | category | flops | bytes accessed | tf_op | source)
XLA Modules:
  0.0 72.5 jit_solution(15809415268343510966)
XLA Ops:
  1.3 1.7 %prepare.1 = (bf16[16,120,128]{2,1,0:T(8,128)(2,1)S(1)}, f32[2,256,128]{2,1,0:T(8,128)S(1)}, bf16[384,128]{1,0:T(8,128)(2,1)S(1)}) custom-call(f32[2]{0:T(128)} %w_hbm.1, s32[1]{0:T(128)S(6)} %copy.8.low_ref, s32[1]{0:T(128)S(6)} %copy.9.high_ref, bf16[2,256,256]{2,1,0:T(8,128)(2,1)} %p_ref.1, bf16[2,256,512]{2,1,0:T(8,128)(2,1)} %b_ref.1, ...), custom_call_target="tpu_custom_call" | custom-call | tf_op jit(solution)/shard_map/prepare/pallas_call | solution.py:337
  3.0 27.4 %all_to_all.15 = bf16[16,120,128]{2,1,0:T(8,128)(2,1)S(1)} all-to-all(bf16[16,120,128]{2,1,0:T(8,128)(2,1)S(1)} %get-tuple-element.10), channel_id=1, replica_groups=mesh['energy'=16,'chip'=16,'core'=2] {'chip'}, dimensions={0} | all-to-all | bytes 983040 | tf_op jit(solution)/shard_map/all_to_all | solution.py:410
  30.5 2.5 %all-gather = bf16[32,120,128]{2,1,0:T(8,128)(2,1)S(1)} all-gather(bf16[16,120,128]{2,1,0:T(8,128)(2,1)S(1)} %all_to_all.15), channel_id=2, replica_groups=mesh['energy'=16,'chip'=16,'core'=2] {'core'}, dimensions={0}, use_global_device_ids=true | all-gather | bytes 1474560 | tf_op jit(solution)/shard_map/all_gather | solution.py:411
  33.0 0.0 copy-start.1
  33.0 4.2 %sweeps.1 = bf16[16,64,128]{2,1,0:T(8,128)(2,1)S(1)} custom-call(bf16[2,16,120,128]{3,2,1,0:T(8,128)(2,1)S(1)} %bitcast.3), custom_call_target="tpu_custom_call" | custom-call | tf_op jit(solution)/shard_map/sweeps/pallas_call | solution.py:363
  37.2 0.0 copy-start
  37.2 14.3 %all_to_all.16 = bf16[16,64,128]{2,1,0:T(8,128)(2,1)S(1)} all-to-all(bf16[16,64,128]{2,1,0:T(8,128)(2,1)S(1)} %sweeps.1), channel_id=1, replica_groups=mesh['energy'=16,'chip'=16,'core'=2] {'chip'}, dimensions={0} | all-to-all | bytes 524288 | tf_op jit(solution)/shard_map/all_to_all | solution.py:413
  51.6 0.0 copy-done.1
  51.6 0.0 copy-done
  51.6 1.1 %finish.1 = bf16[16,16,256]{2,1,0:T(8,128)(2,1)S(1)} custom-call(f32[2,256,128]{2,1,0:T(8,128)S(1)} %get-tuple-element.8.scale_ref, bf16[384,128]{1,0:T(8,128)(2,1)S(1)} %get-tuple-element.9.front_ref, bf16[2,256,256]{2,1,0:T(8,128)(2,1)S(1)} %copy-done.1, bf16[2,256,512]{2,1,0:T(8,128)(2,1)S(1)} %copy-done, bf16[2,512,128]{2,1,0:T(8,128)(2,1)S(1)} %bitcast.4), custom_call_target="tpu_custom_call" | custom-call | tf_op jit(solution)/shard_map/finish/pallas_call | solution.py:380
  52.7 19.2 %all_to_all.17 = bf16[16,16,256]{2,1,0:T(8,128)(2,1)S(1)} all-to-all(bf16[16,16,256]{2,1,0:T(8,128)(2,1)S(1)} %finish.1), channel_id=1, replica_groups=mesh['energy'=16,'chip'=16,'core'=2] {'energy'}, dimensions={0} | all-to-all | bytes 262144 | tf_op jit(solution)/shard_map/all_to_all | solution.py:423
  71.9 0.6 convert_reduce_fusion
Async XLA Ops:
  33.0 18.6 %copy-start.1 = (bf16[2,256,256]{2,1,0:T(8,128)(2,1)S(1)}, bf16[2,256,256]{2,1,0:T(8,128)(2,1)}, u32[]{:S(2)}) copy-start(bf16[2,256,256]{2,1,0:T(8,128)(2,1)} %p_ref.1) | copy-start | bytes 786436
  37.2 14.4 %copy-start = (bf16[2,256,512]{2,1,0:T(8,128)(2,1)S(1)}, bf16[2,256,512]{2,1,0:T(8,128)(2,1)}, u32[]{:S(2)}) copy-start(bf16[2,256,512]{2,1,0:T(8,128)(2,1)} %b_ref.1) | copy-start | bytes 1572868
